TPU v7x, 32 devices: a whole 2x2x4 slice. The times are simulated.
32 devices in a mesh: row: 8 (over z, x), col: 4 (over y, core).
Axes of the slice: x: 2, y: 2, z: 4, core: 2. Of those that a mesh axis runs over, the one named last changes fastest.
Arguments:
- features: bfloat16 [4096, 128], P(('row', 'col')), may hold values from -6 to 6
- cotangent: bfloat16 [4096, 128], P(('row', 'col')), may hold values from -6 to 6
- self_weight: bfloat16 [128, 128], replicated, may hold values from -0.5 to 0.5
- neigh_weight: bfloat16 [128, 128], replicated, may hold values from -0.5 to 0.5
- degrees: int32 [4096], P(('row', 'col')), may hold values from 512 to 2048
- adjacency: int32 [8, 4, 64, 128, 128], P('row', 'col'), may hold values 0 or 1
- tile_rows: int32 [8, 4, 64], P('row', 'col'), may hold values from 0 to 7
- tile_cols: int32 [8, 4, 64], P('row', 'col'), may hold values from 0 to 3
- tile_count: int32 [8, 4], P('row', 'col'), may hold values from 32 to 64, as said below
Outputs:
- hidden: bfloat16 [4096, 128], P(('row', 'col'))
- grad_features: bfloat16 [4096, 128], P(('row', 'col'))
- grad_self: float32 [128, 128], replicated
- grad_neigh: float32 [128, 128], replicated
Inputs may be any that keep to these rules, and one draw needn't show every extreme that they name: `tile_count`: each device has between 64 // 2 (at least 1) and 64 live slots; in every draw some device has exactly 64. `tile_rows`: only a device's first tile_count slots are live; places may repeat. `tile_cols`: only a device's first tile_count slots are live; places may repeat.
All inputs are finite; a program needn't handle non-finite values. No bound on the sum of `adjacency` on one device may be relied on, other than what follows from the above.
Results may differ from a plain program's by a relative error of at most 0.024.
Values may be sent and summed in bfloat16 or wider, within the bound.
A program may use at most 64 MiB of HBM per device.

v0:
```python
import jax
import jax.numpy as jnp
from jax import lax
from jax.sharding import PartitionSpec as P


def tile_sums(tile_bits, pick_blocks, place_blocks, is_live, source, out_blocks, transpose):
    edge = tile_bits.shape[-1]
    source_blocks = source.reshape(-1, edge, source.shape[-1])
    chosen = jnp.take(source_blocks, pick_blocks, axis=0)
    if transpose:
        products = jnp.einsum("kji,kjf->kif", tile_bits, chosen, preferred_element_type=jnp.float32)
    else:
        products = jnp.einsum("kij,kjf->kif", tile_bits, chosen, preferred_element_type=jnp.float32)
    targets = jnp.arange(out_blocks, dtype=jnp.int32)
    select = jnp.where(
        (place_blocks[None, :] == targets[:, None]) & is_live[None, :], 1.0, 0.0
    ).astype(jnp.float32)
    summed = jnp.einsum("bk,kif->bif", select, products, precision=lax.Precision.HIGHEST)
    return summed.reshape(out_blocks * edge, source.shape[-1])


def dense_layer(node_feats, node_cot, mixed, self_weight, neigh_weight, inverse):
    linear = jnp.dot(node_feats, self_weight, preferred_element_type=jnp.float32) + jnp.dot(
        mixed, neigh_weight, preferred_element_type=jnp.float32
    )
    sigma = jax.nn.sigmoid(linear)
    hidden = (linear * sigma).astype(jnp.bfloat16)
    grad_linear = (node_cot.astype(jnp.float32) * sigma * (1.0 + linear * (1.0 - sigma))).astype(
        jnp.bfloat16
    )
    grad_mixed = (
        jnp.dot(grad_linear, neigh_weight.T, preferred_element_type=jnp.float32) * inverse
    ).astype(jnp.bfloat16)
    return (hidden, grad_linear, grad_mixed)


def body(
    features,
    cotangent,
    self_weight,
    neigh_weight,
    degrees,
    adjacency,
    tile_rows,
    tile_cols,
    tile_count,
):
    edge = adjacency.shape[-1]
    capacity = adjacency.shape[2]
    tile_bits = adjacency.reshape(capacity, edge, edge).astype(jnp.bfloat16)
    row_ids = tile_rows.reshape(capacity)
    col_ids = tile_cols.reshape(capacity)
    is_live = jnp.arange(capacity, dtype=jnp.int32) < tile_count.reshape(())
    owned = features.shape[0]
    row_blocks = lax.axis_size("row") * owned // edge
    col_blocks = lax.axis_size("col") * owned // edge
    inverse = lax.rsqrt(jnp.maximum(degrees, 1).astype(jnp.float32))[:, None]
    source = lax.all_gather(features, "col", axis=0, tiled=True)
    partial_value = tile_sums(
        tile_bits, col_ids, row_ids, is_live, source, row_blocks, False
    ).astype(jnp.bfloat16)
    summed = lax.psum_scatter(partial_value, "row", scatter_dimension=0, tiled=True).astype(
        jnp.float32
    )
    mixed = (summed * inverse).astype(jnp.bfloat16)
    hidden, grad_linear, grad_mixed = dense_layer(
        features, cotangent, mixed, self_weight, neigh_weight, inverse
    )
    spread = lax.all_gather(grad_mixed, "row", axis=0, tiled=True)
    back_partial = tile_sums(tile_bits, row_ids, col_ids, is_live, spread, col_blocks, True).astype(
        jnp.bfloat16
    )
    returned = lax.psum_scatter(back_partial, "col", scatter_dimension=0, tiled=True).astype(
        jnp.float32
    )
    grad_features = (
        jnp.dot(grad_linear, self_weight.T, preferred_element_type=jnp.float32) + returned
    ).astype(jnp.bfloat16)
    local_self = jnp.einsum("nf,ng->fg", features, grad_linear, preferred_element_type=jnp.float32)
    local_neigh = jnp.einsum("nf,ng->fg", mixed, grad_linear, preferred_element_type=jnp.float32)
    grad_self, grad_neigh = lax.psum((local_self, local_neigh), ("row", "col"))
    return (hidden, grad_features, grad_self, grad_neigh)


def solution(mesh):
    in_specs = (
        P(("row", "col"), None),
        P(("row", "col"), None),
        P(),
        P(),
        P(("row", "col")),
        P("row", "col", None, None, None),
        P("row", "col", None),
        P("row", "col", None),
        P("row", "col"),
    )
    out_specs = (P(("row", "col"), None), P(("row", "col"), None), P(), P())
    return jax.shard_map(body, mesh=mesh, in_specs=in_specs, out_specs=out_specs, check_vma=False)
```

profile of v0, /device:TPU:0, one launch (start us, length us, event | category | flops | bytes accessed | tf_op | source)
XLA Modules:
  0.0 294.8 jit_solution(9851841026771200526)
XLA Ops:
  7.2 0.0 copy-start
  7.2 0.0 reduce-scatter.3.cloned.1.call-start
  7.2 0.7 fusion.41
  7.9 0.7 compare_and_fusion.1
  8.5 6.7 %all_gather.6 = bf16[512,128]{1,0:T(8,128)(2,1)S(1)} all-gather(bf16[128,128]{1,0:T(8,128)(2,1)} %param.9), channel_id=1, replica_groups=mesh['row'=8,'col'=4] {'col'}, dimensions={0}, use_global_device_ids=true | all-gather | bytes 163840 | tf_op jit(solution)/shard_map/all_gather | solution.py:59
  15.3 0.9 gather_fusion
  16.2 5.9 %fusion.6 = f32[64,128,128]{2,1,0:T(8,128)} fusion(bf16[64,128,128]{2,1,0:T(8,128)(2,1)S(1)} %gather_fusion, pred[64]{0:T(512)(128)(4,1)S(1)} %compare_and_fusion.1, s32[1,1,64,128,128]{4,3,2,1,0:T(8,128)} %param.14), kind=kOutput, calls=%fused_computation.8 | convolution fusion | flops 270532608 | bytes 10485824 | tf_op jit(solution)/shard_map/kij,kjf->kif/dot_general | solution.py:14
  22.1 5.4 %copy.18 = f32[64,128,128]{1,0,2:T(8,128)} copy(f32[64,128,128]{2,1,0:T(8,128)} %fusion.6) | data formatting | bytes 8388608 | tf_op jit(solution)/shard_map/kij,kjf->kif/dot_general | solution.py:14
  28.3 4.3 %fusion.12 = bf16[8,128,128]{2,0,1:T(8,128)(2,1)S(1)} fusion(f32[64,128,128]{1,0,2:T(8,128)} %copy.18, s32[64]{0:T(128)S(1)} %bitcast.55, pred[64]{0:T(512)(128)(4,1)S(1)} %iota_compare_fusion.2), kind=kOutput, calls=%fused_computation.14 | convolution fusion | flops 100795904 | bytes 4456768 | tf_op jit(solution)/shard_map/bk,kif->bif/dot_general | solution.py:19
  32.5 0.8 copy.15
  33.3 0.0 reduce-scatter.3.cloned.1.call-update
  33.3 0.0 all-reduce.3.cloned.1.call-start
  33.4 0.1 fusion.49
  33.6 62.7 %reduce-scatter.3.cloned.1.call-done = bf16[128,128]{1,0:T(8,128)(2,1)} async-done(((bf16[1024,128]{1,0:T(8,128)(2,1)}), bf16[128,128]{1,0:T(8,128)(2,1)}) %reduce-scatter.3.cloned.1.call-update) | async-done | bytes 32784 | tf_op jit(solution)/shard_map/reduce_scatter | solution.py:63
  96.3 1.6 multiply_convert_fusion
  97.9 0.1 fusion.19
  98.0 0.9 convolution_bitcast_fusion
  98.9 30.9 %all_gather.7 = bf16[1024,128]{1,0:T(8,128)(2,1)S(1)} all-gather(bf16[128,128]{1,0:T(8,128)(2,1)S(1)} %fusion.19), channel_id=1, replica_groups=mesh['row'=8,'col'=4] {'row'}, dimensions={0}, use_global_device_ids=true | all-gather | bytes 294912 | tf_op jit(solution)/shard_map/all_gather | solution.py:70
  129.7 0.9 gather_fusion.1
  130.7 5.1 %fusion.4 = f32[64,128,128]{2,1,0:T(8,128)} fusion(bf16[64,128,128]{2,1,0:T(8,128)(2,1)S(1)} %gather_fusion.1, pred[64]{0:T(512)(128)(4,1)S(1)} %compare_and_fusion, s32[1,1,64,128,128]{4,3,2,1,0:T(8,128)} %param.14), kind=kOutput, calls=%fused_computation.6 | convolution fusion | flops 270532608 | bytes 10485824 | tf_op jit(solution)/shard_map/kji,kjf->kif/dot_general | solution.py:12
  135.8 5.4 %copy.19 = f32[64,128,128]{1,0,2:T(8,128)} copy(f32[64,128,128]{2,1,0:T(8,128)} %fusion.4) | data formatting | bytes 8388608 | tf_op jit(solution)/shard_map/kji,kjf->kif/dot_general | solution.py:12
  141.2 0.9 fusion.24
  142.1 0.0 all-reduce.3.cloned.1.call-update
  142.1 0.0 reduce-scatter.5.cloned.1.call-start
  142.2 4.3 %fusion.15 = bf16[4,128,128]{2,0,1:T(4,128)(2,1)S(1)} fusion(f32[64,128,128]{1,0,2:T(8,128)} %copy.19, s32[64]{0:T(128)S(1)} %bitcast.56, pred[64]{0:T(512)(128)(4,1)S(1)} %iota_compare_fusion.2), kind=kOutput, calls=%fused_computation.15 | convolution fusion | flops 50397952 | bytes 4325696 | tf_op jit(solution)/shard_map/bk,kif->bif/dot_general | solution.py:19
  146.5 0.7 copy.16
  147.1 0.0 reduce-scatter.5.cloned.1.call-update
  147.1 117.0 %all-reduce.3.cloned.1.call-done = (f32[128,128]{0,1:T(8,128)}, f32[128,128]{1,0:T(8,128)}) async-done(((f32[128,128]{0,1:T(8,128)}, f32[128,128]{1,0:T(8,128)}), (f32[128,128]{0,1:T(8,128)}, f32[128,128]{1,0:T(8,128)})) %all-reduce.3.cloned.1.call-update) | async-done | bytes 131088 | tf_op jit(solution)/shard_map/psum | solution.py:82
  264.2 1.6 copy.17
  265.8 19.5 %reduce-scatter.5.cloned.1.call-done = bf16[128,128]{1,0:T(8,128)(2,1)} async-done(((bf16[512,128]{1,0:T(8,128)(2,1)}), bf16[128,128]{1,0:T(8,128)(2,1)}) %reduce-scatter.5.cloned.1.call-update) | async-done | bytes 32784 | tf_op jit(solution)/shard_map/reduce_scatter | solution.py:74
  285.2 1.5 fusion.18
  286.8 1.5 copy.23
  (21 shorter events, 0.1 us)
Async XLA Ops:
  7.2 89.1 %copy-start = (bf16[128,128]{1,0:T(8,128)(2,1)S(1)}, bf16[128,128]{1,0:T(8,128)(2,1)}, u32[]{:S(2)}) copy-start(bf16[128,128]{1,0:T(8,128)(2,1)} %param.12) | copy-start | bytes 98308
  7.2 89.1 %reduce-scatter.3.cloned.1.call-start = ((), (), s32[]{:S(2)}) async-start(), calls=%async_computation.2 | async-start | bytes 294912 | tf_op jit(solution)/shard_map/reduce_scatter | solution.py:63
  22.1 6.1 %copy-start.4 = (s32[1,1,64]{2,1,0:T(1,128)S(1)}, s32[1,1,64]{2,1,0:T(1,128)}, u32[]{:S(2)}) copy-start(s32[1,1,64]{2,1,0:T(1,128)} %param.15) | copy-start | bytes 772
  28.2 5.2 %copy-start.7 = (s32[128]{0:T(128)S(1)}, s32[128]{0:T(128)}, u32[]{:S(2)}) copy-start(s32[128]{0:T(128)} %param.13) | copy-start | bytes 1540
  28.2 5.2 %copy-start.1 = (bf16[128,128]{1,0:T(8,128)(2,1)S(1)}, bf16[128,128]{1,0:T(8,128)(2,1)}, u32[]{:S(2)}) copy-start(bf16[128,128]{1,0:T(8,128)(2,1)} %param.9) | copy-start | bytes 98308
  28.2 5.2 %copy-start.2 = (bf16[128,128]{1,0:T(8,128)(2,1)S(1)}, bf16[128,128]{1,0:T(8,128)(2,1)}, u32[]{:S(2)}) copy-start(bf16[128,128]{1,0:T(8,128)(2,1)} %param.11) | copy-start | bytes 98308
  28.3 68.0 %copy-start.6 = (bf16[128,128]{1,0:T(8,128)(2,1)S(1)}, bf16[128,128]{1,0:T(8,128)(2,1)}, u32[]{:S(2)}) copy-start(bf16[128,128]{1,0:T(8,128)(2,1)} %param.10) | copy-start | bytes 98308
  33.3 230.9 %all-reduce.3.cloned.1.call-start = ((), (), s32[]{:S(2)}) async-start(), calls=%async_computation.4 | async-start | bytes 262144 | tf_op jit(solution)/shard_map/psum | solution.py:82
  135.8 5.4 %copy-start.3 = (bf16[128,128]{1,0:T(8,128)(2,1)S(1)}, bf16[128,128]{1,0:T(8,128)(2,1)}, u32[]{:S(2)}) copy-start(bf16[128,128]{1,0:T(8,128)(2,1)} %reduce-scatter.3.cloned.1.call-done) | copy-start | bytes 98308
  135.8 6.4 %copy-start.5 = (s32[1,1,64]{2,1,0:T(1,128)S(1)}, s32[1,1,64]{2,1,0:T(1,128)}, u32[]{:S(2)}) copy-start(s32[1,1,64]{2,1,0:T(1,128)} %param.16) | copy-start | bytes 772
  142.1 143.1 %reduce-scatter.5.cloned.1.call-start = ((), (), s32[]{:S(2)}) async-start(), calls=%async_computation.3 | async-start | bytes 163840 | tf_op jit(solution)/shard_map/reduce_scatter | solution.py:74
Sparse Core Ops, SparseCore 0:
  33.4 62.8 reduce-scatter.2
  142.3 121.8 all-reduce.2
  266.6 18.5 reduce-scatter.4
where the time goes:
time: 295 us
  waiting for transfers between devices  199 us (67%)
  blocking collectives  37.6 us (13%)
  matrix products  24.7 us (8%)
  local copies, waits for them, and re-layouts  17.2 us (6%)
  between operations  14.5 us (5%)
    psum x1, waiting for transfers between devices, body(): grad_self, grad_neigh = lax.psum((local_self, local_neigh), ('row', 'col'))  117 us
    reduce_scatter x1, waiting for transfers between devices, body(): lax.psum_scatter(partial_value, 'row', scatter_dimension=0, tiled=True)  62.7 us
    all_gather x1, blocking collectives, body(): spread = lax.all_gather(grad_mixed, 'row', axis=0, tiled=True)  30.9 us
    reduce_scatter x1, waiting for transfers between devices, body(): lax.psum_scatter(back_partial, 'col', scatter_dimension=0, tiled=True)  19.5 us
    dot_general x2, matrix products, tile_sums(): jnp.einsum('bk,kif->bif', select, products, precision=lax.Precision.HIGHEST)  8.53 us
    all_gather x1, blocking collectives, body(): source = lax.all_gather(features, 'col', axis=0, tiled=True)  6.71 us
    dot_general x1, matrix products, tile_sums(): jnp.einsum('kij,kjf->kif', tile_bits, chosen, preferred_element_type=jnp....  5.92 us
  transfers between devices with their start and end apart: 3, of which 3 were waited for; matrix products, arithmetic and copies ran while one was open for 2% of the time, Pallas kernels for 0%

commit v1 on v0

v1 whole, which is shorter than its diff:
```python
import functools

import jax
import jax.numpy as jnp
from jax import lax
from jax.experimental import pallas as pl
from jax.experimental.pallas import tpu as pltpu
from jax.sharding import PartitionSpec as P

MESH = pl.DeviceIdType.MESH
BF16 = jnp.bfloat16
F32 = jnp.float32
CHUNK = 8


def dot(a, b, contract=((1,), (0,))):
    return lax.dot_general(a, b, (contract, ((), ())), preferred_element_type=F32)


def each(low, high, step):
    if high - low <= 8:
        for index in range(low, high):
            step(index)
    else:
        def looped(index, carry):
            step(index)
            return carry
        lax.fori_loop(low, high, looped, 0)


def place_kernel(chunks, count_ref, rows_ref, cols_ref, tiles_hbm, dense_ref, tiles, sems):
    edge = tiles.shape[-1]
    copies = []
    for index in range(chunks):
        piece = pl.ds(index * CHUNK, CHUNK)
        copy = pltpu.make_async_copy(tiles_hbm.at[piece], tiles.at[piece], sems.at[index])
        copy.start()
        copies.append(copy)
    count = count_ref[0, 0]
    dense_ref[...] = jnp.zeros_like(dense_ref)
    for index in range(chunks):
        copies[index].wait()

        def place(slot, carry):
            row = pl.multiple_of(rows_ref[0, slot] * edge, edge)
            col = pl.multiple_of(cols_ref[0, slot] * edge, edge)
            spot = (pl.ds(row, edge), pl.ds(col, edge))
            dense_ref[spot] = dense_ref[spot] + tiles[slot].astype(F32).astype(BF16)
            return carry

        first = index * CHUNK
        last = jnp.clip(count, first, first + CHUNK)
        lax.fori_loop(first, last, place, 0)


def layer_kernel(
    n_row, n_col,
    feat_ref, cot_ref, self_ref, neigh_ref, deg_ref, dense_hbm,
    hidden_ref, gfeat_ref, gself_ref, gneigh_ref,
    dense, src, part_out, part_in, gm, back_out, back_in, w_out, w_in, q_out, q_in, fin, back_acc,
    dense_sem, src_s, src_r, part_s, part_r, gm_s, gm_r, back_s, back_r,
    w_s, w_r, q_s, q_r, fin_s, fin_r,
):
    r = lax.axis_index("row")
    c = lax.axis_index("col")
    edge = feat_ref.shape[0]

    def row_at(d):
        return lax.rem(r + d, n_row)

    def col_at(d):
        return lax.rem(c + d, n_col)

    def over_row(source, target, send, recv, d):
        return pltpu.make_async_remote_copy(
            src_ref=source, dst_ref=target, send_sem=send.at[d], recv_sem=recv.at[d],
            device_id=(row_at(d), c), device_id_type=MESH)

    def over_col(source, target, send, recv, d):
        return pltpu.make_async_remote_copy(
            src_ref=source, dst_ref=target, send_sem=send.at[d], recv_sem=recv.at[d],
            device_id=(r, col_at(d)), device_id_type=MESH)

    fetch = pltpu.make_async_copy(dense_hbm, dense, dense_sem)
    fetch.start()
    barrier = pltpu.get_barrier_semaphore()
    each(1, n_col, lambda d: pl.semaphore_signal(
        barrier, inc=1, device_id=(r, col_at(d)), device_id_type=MESH))
    each(1, n_row, lambda d: pl.semaphore_signal(
        barrier, inc=1, device_id=(row_at(d), c), device_id_type=MESH))
    pl.semaphore_wait(barrier, n_row + n_col - 2)

    def src_copy(d):
        return over_col(feat_ref, src.at[c], src_s, src_r, d)

    each(1, n_col, lambda d: src_copy(d).start())
    keep = pltpu.make_async_copy(feat_ref, src.at[c], src_r.at[0])
    keep.start()
    inv_row = lax.rsqrt(jnp.maximum(deg_ref[...], 1).astype(F32))
    down = lax.broadcasted_iota(jnp.int32, (edge, edge), 0)
    across = lax.broadcasted_iota(jnp.int32, (edge, edge), 1)
    inv_col = jnp.sum(jnp.where(down == across, inv_row, 0.0), axis=1, keepdims=True)
    own_linear = dot(feat_ref[...], self_ref[...])
    fetch.wait()
    keep.wait()
    each(1, n_col, lambda d: src_copy(d).wait_recv())
    source = src[...].reshape(n_col * edge, src.shape[-1])

    def part_copy(d):
        return over_row(part_out.at[d], part_in.at[d], part_s, part_r, d)

    def partial(d):
        rows = pl.ds(pl.multiple_of(row_at(d) * edge, edge), edge)
        return dot(dense[rows, :], source)

    def send_part(d):
        part_out[d] = partial(d).astype(BF16)
        part_copy(d).start()

    each(1, n_row, send_part)
    agg = partial(0).astype(BF16).astype(F32)
    for d in range(1, n_row):
        part_copy(d).wait_recv()
        agg = agg + part_in[d].astype(F32)

    mixed = (agg * inv_col).astype(BF16)
    linear = own_linear + dot(mixed, neigh_ref[...])
    sigma = jax.nn.sigmoid(linear)
    slope = sigma * (1.0 + linear * (1.0 - sigma))
    grad_linear = (cot_ref[...].astype(F32) * slope).astype(BF16)
    gm[r] = (dot(neigh_ref[...], grad_linear, ((1,), (1,))) * inv_row).astype(BF16)

    def gm_copy(d):
        return over_row(gm.at[r], gm.at[r], gm_s, gm_r, d)

    each(1, n_row, lambda d: gm_copy(d).start())

    share = w_out.shape[1]
    both = jnp.concatenate([feat_ref[...], mixed], axis=1)
    w_out[...] = dot(both, grad_linear, ((0,), (0,))).reshape(w_out.shape)

    def w_copy(d):
        return over_col(w_out.at[col_at(d)], w_in.at[d], w_s, w_r, d)

    each(1, n_col, lambda d: w_copy(d).start())
    hidden_ref[...] = (linear * sigma).astype(BF16)
    own_grad = dot(grad_linear, self_ref[...], ((1,), (1,)))

    def q_copy(d):
        return over_row(q_out, q_in.at[d], q_s, q_r, d)

    def sum_over_col():
        total = w_out[c]
        for d in range(1, n_col):
            w_copy(d).wait_recv()
            total = total + w_in[d]
        q_out[...] = total.astype(BF16)
        each(1, n_row, lambda d: q_copy(d).start())
        return total

    def back_term(d):
        owner = lax.rem(r - d + n_row, n_row)
        rows = pl.ds(pl.multiple_of(owner * edge, edge), edge)
        return dot(gm[owner], dense[rows, :])

    def add_back(d):
        gm_copy(d).wait_recv()
        back_acc[...] += back_term(d)

    middle = (n_row + 1) // 2
    back_acc[...] = back_term(0)
    each(1, middle, add_back)
    total = sum_over_col()
    each(middle, n_row, add_back)

    for b in range(n_col):
        back_out[b] = back_acc[:, b * edge:(b + 1) * edge].astype(BF16)

    def back_copy(d):
        return over_col(back_out.at[col_at(d)], back_in.at[d], back_s, back_r, d)

    each(1, n_col, lambda d: back_copy(d).start())

    for d in range(1, n_row):
        q_copy(d).wait_recv()
        total = total + q_in[d].astype(F32)
    fin[c] = total.astype(BF16)

    def fin_copy(d):
        return over_col(fin.at[c], fin.at[c], fin_s, fin_r, d)

    each(1, n_col, lambda d: fin_copy(d).start())

    returned = back_out[c].astype(F32)
    for d in range(1, n_col):
        back_copy(d).wait_recv()
        returned = returned + back_in[d].astype(F32)
    gfeat_ref[...] = (own_grad + returned.T).astype(BF16)

    each(1, n_col, lambda d: fin_copy(d).wait_recv())
    grads = fin[...].reshape(n_col * share, fin.shape[-1]).astype(F32)
    half = gself_ref.shape[0]
    gself_ref[...] = grads[:half]
    gneigh_ref[...] = grads[half:]

    def drain_col(d):
        for copy in (src_copy, w_copy, back_copy, fin_copy):
            copy(d).wait_send()

    def drain_row(d):
        for copy in (part_copy, gm_copy, q_copy):
            copy(d).wait_send()

    each(1, n_col, drain_col)
    each(1, n_row, drain_row)


def body(n_row, n_col, features, cotangent, self_weight, neigh_weight, degrees,
         adjacency, tile_rows, tile_cols, tile_count):
    edge = adjacency.shape[-1]
    capacity = adjacency.shape[2]
    hidden_units = features.shape[-1]
    chunks = capacity // CHUNK
    rows, cols = n_row * edge, n_col * edge
    smem = pl.BlockSpec(memory_space=pltpu.SMEM)
    vmem = pl.BlockSpec(memory_space=pltpu.VMEM)
    anywhere = pl.BlockSpec(memory_space=pl.ANY)
    dense = pl.pallas_call(
        functools.partial(place_kernel, chunks),
        out_shape=jax.ShapeDtypeStruct((rows, cols), BF16),
        in_specs=[smem, smem, smem, anywhere],
        out_specs=vmem,
        scratch_shapes=[
            pltpu.VMEM((capacity, edge, edge), jnp.int32),
            pltpu.SemaphoreType.DMA((chunks,)),
        ],
        compiler_params=pltpu.CompilerParams(vmem_limit_bytes=60 * 2**20),
        name="place_tiles",
    )(
        tile_count.reshape(1, 1),
        tile_rows.reshape(1, capacity),
        tile_cols.reshape(1, capacity),
        adjacency.reshape(capacity, edge, edge),
    )
    share = 2 * hidden_units // n_col
    block = (edge, hidden_units)
    dma = pltpu.SemaphoreType.DMA
    return pl.pallas_call(
        functools.partial(layer_kernel, n_row, n_col),
        out_shape=(
            jax.ShapeDtypeStruct(block, BF16),
            jax.ShapeDtypeStruct(block, BF16),
            jax.ShapeDtypeStruct(self_weight.shape, F32),
            jax.ShapeDtypeStruct(neigh_weight.shape, F32),
        ),
        in_specs=[vmem] * 5 + [anywhere],
        out_specs=(vmem,) * 4,
        scratch_shapes=[
            pltpu.VMEM((rows, cols), BF16),
            pltpu.VMEM((n_col,) + block, BF16),
            pltpu.VMEM((n_row,) + block, BF16),
            pltpu.VMEM((n_row,) + block, BF16),
            pltpu.VMEM((n_row,) + block, BF16),
            pltpu.VMEM((n_col,) + block, BF16),
            pltpu.VMEM((n_col,) + block, BF16),
            pltpu.VMEM((n_col, share, hidden_units), F32),
            pltpu.VMEM((n_col, share, hidden_units), F32),
            pltpu.VMEM((share, hidden_units), BF16),
            pltpu.VMEM((n_row, share, hidden_units), BF16),
            pltpu.VMEM((n_col, share, hidden_units), BF16),
            pltpu.VMEM((hidden_units, cols), F32),
            dma,
            dma((n_col,)), dma((n_col,)),
            dma((n_row,)), dma((n_row,)),
            dma((n_row,)), dma((n_row,)),
            dma((n_col,)), dma((n_col,)),
            dma((n_col,)), dma((n_col,)),
            dma((n_row,)), dma((n_row,)),
            dma((n_col,)), dma((n_col,)),
        ],
        compiler_params=pltpu.CompilerParams(
            collective_id=0, has_side_effects=True, vmem_limit_bytes=48 * 2**20),
        name="layer_exchange",
    )(features, cotangent, self_weight, neigh_weight, degrees.reshape(1, edge), dense)


def solution(mesh):
    in_specs = (
        P(("row", "col"), None),
        P(("row", "col"), None),
        P(),
        P(),
        P(("row", "col")),
        P("row", "col", None, None, None),
        P("row", "col", None),
        P("row", "col", None),
        P("row", "col"),
    )
    out_specs = (P(("row", "col"), None), P(("row", "col"), None), P(), P())
    n_row, n_col = mesh.shape["row"], mesh.shape["col"]
    return jax.shard_map(functools.partial(body, n_row, n_col), mesh=mesh,
                         in_specs=in_specs, out_specs=out_specs, check_vma=False)
```

time: 295 us -> 42.4 us (0.14)
  waiting for transfers between devices: 199 us -> 0 us
  blocking collectives: 37.6 us -> 0 us
  Pallas kernels: 0 us -> 37 us
  matrix products: 24.7 us -> 0 us
  local copies, waits for them, and re-layouts: 17.2 us -> 3.73 us
  between operations: 14.5 us -> 1.41 us
    psum x1 -> x0, waiting for transfers between devices: 117 us -> none  [body(): grad_self, grad_neigh = lax.psum((local_self, local_neigh), ('row', 'col'))]
    reduce_scatter x2 -> x0, waiting for transfers between devices: 82.2 us -> none  [the longest x1 62.7 us: body(): lax.psum_scatter(partial_value, 'row', scatter_dimension=0, tiled=True)]
    all_gather x2 -> x0, blocking collectives: 37.6 us -> none  [the longest x1 30.9 us: body(): spread = lax.all_gather(grad_mixed, 'row', axis=0, tiled=True)]
    pallas_call x0 -> x2, Pallas kernels: none -> 37 us  [the longest x1 33.1 us: body(): pl.pallas_call(functools.partial(layer_kernel, n_row, n_col), out_shape=(...]
    dot_general x10 -> x0, matrix products: 24.7 us -> none  [the longest x2 8.53 us: tile_sums(): jnp.einsum('bk,kif->bif', select, products, precision=lax.Precision.HIGHEST)]
    dot_general x2 -> x0, local copies, waits for them, and re-layouts: 10.8 us -> none  [the longest x1 5.41 us: tile_sums(): jnp.einsum('kji,kjf->kif', tile_bits, chosen, preferred_element_type=jnp....]
  transfers between devices with their start and end apart: 3 -> 0, of which waited for: 3 -> 0; matrix products, arithmetic and copies ran while one was open for 2% -> 0% of each run, Pallas kernels for 0% -> 0%
where the time goes in v1:
time: 42.4 us; the launch traced here: 42.1 us
  Pallas kernels  37 us (87%)
  local copies, waits for them, and re-layouts  3.73 us (9%)
  between operations  1.41 us (3%)
    pallas_call x1, Pallas kernels, body(): pl.pallas_call(functools.partial(layer_kernel, n_row, n_col), out_shape=(...  33.1 us
    pallas_call x1, Pallas kernels, body(): pl.pallas_call(functools.partial(place_kernel, chunks), out_shape=jax.Sha...  3.93 us
    unnamed x16, local copies, waits for them, and re-layouts  3.73 us

profile of v1, /device:TPU:0, one launch (start us, length us, event | category | flops | bytes accessed | tf_op | source)
XLA Modules:
  0.0 42.1 jit_solution(4384427944887578331)
XLA Ops:
  0.6 0.0 copy-start.5
  0.6 0.0 copy-start.4
  0.7 0.0 copy-start.3
  0.7 0.0 copy-start.2
  0.7 0.0 copy-start.1
  1.4 3.9 %place_tiles.1.dense_hbm = bf16[1024,512]{1,0:T(8,128)(2,1)} custom-call(s32[1,1]{1,0:T(1,128)S(6)} %copy.17.count_ref, s32[1,64]{1,0:T(1,128)} %bitcast.6, s32[1,64]{1,0:T(1,128)} %bitcast.7, s32[64,128,128]{2,1,0:T(8,128)} %bitcast.5), custom_call_target="tpu_custom_call" | custom-call | tf_op jit(solution)/shard_map/place_tiles/pallas_call | solution.py:228
  5.3 0.0 copy-done.5
  5.3 0.0 copy-done.4
  5.3 0.0 copy-done.3
  5.3 0.0 copy-done.2
  5.3 0.0 copy-done.1
  5.3 0.0 copy-start
  5.4 1.2 %copy-done = bf16[1024,512]{1,0:T(8,128)(2,1)S(1)} copy-done((bf16[1024,512]{1,0:T(8,128)(2,1)S(1)}, bf16[1024,512]{1,0:T(8,128)(2,1)}, u32[]{:S(2)}) %copy-start) | copy-done | bytes 1048600
  6.6 33.1 %layer_exchange.1 = (bf16[128,128]{1,0:T(8,128)(2,1)S(1)}, bf16[128,128]{1,0:T(8,128)(2,1)S(1)}, f32[128,128]{1,0:T(8,128)S(1)}, f32[128,128]{1,0:T(8,128)S(1)}) custom-call(bf16[128,128]{1,0:T(8,128)(2,1)S(1)} %copy-done.1, bf16[128,128]{1,0:T(8,128)(2,1)S(1)} %copy-done.2, bf16[128,128]{1,0:T(8,128)(2,1)S(1)} %copy-done.3, bf16[128,128]{1,0:T(8,128)(2,1)S(1)} %copy-done.4, ...), custom_call_target="tpu_custom_call" | custom-call | tf_op jit(solution)/shard_map/layer_exchange/pallas_call | solution.py:248
  39.6 0.6 %copy.18 = bf16[128,128]{1,0:T(8,128)(2,1)} copy(bf16[128,128]{1,0:T(8,128)(2,1)S(1)} %get-tuple-element.8) | data formatting | bytes 65536
  40.3 0.6 %copy.19 = bf16[128,128]{1,0:T(8,128)(2,1)} copy(bf16[128,128]{1,0:T(8,128)(2,1)S(1)} %get-tuple-element.9) | data formatting | bytes 65536
  40.9 0.6 %copy.20 = f32[128,128]{1,0:T(8,128)} copy(f32[128,128]{1,0:T(8,128)S(1)} %get-tuple-element.10) | data formatting | bytes 131072
  41.5 0.6 %copy.21 = f32[128,128]{1,0:T(8,128)} copy(f32[128,128]{1,0:T(8,128)S(1)} %get-tuple-element.11) | data formatting | bytes 131072
Async XLA Ops:
  0.6 4.7 %copy-start.5 = (s32[128]{0:T(128)S(1)}, s32[128]{0:T(128)}, u32[]{:S(2)}) copy-start(s32[128]{0:T(128)} %param.13) | copy-start | bytes 1540
  0.6 4.7 %copy-start.4 = (bf16[128,128]{1,0:T(8,128)(2,1)S(1)}, bf16[128,128]{1,0:T(8,128)(2,1)}, u32[]{:S(2)}) copy-start(bf16[128,128]{1,0:T(8,128)(2,1)} %neigh_ref.1) | copy-start | bytes 98308
  0.7 4.7 %copy-start.3 = (bf16[128,128]{1,0:T(8,128)(2,1)S(1)}, bf16[128,128]{1,0:T(8,128)(2,1)}, u32[]{:S(2)}) copy-start(bf16[128,128]{1,0:T(8,128)(2,1)} %self_ref.1) | copy-start | bytes 98308
  0.7 4.7 %copy-start.2 = (bf16[128,128]{1,0:T(8,128)(2,1)S(1)}, bf16[128,128]{1,0:T(8,128)(2,1)}, u32[]{:S(2)}) copy-start(bf16[128,128]{1,0:T(8,128)(2,1)} %cot_ref.1) | copy-start | bytes 98308
  0.7 4.7 %copy-start.1 = (bf16[128,128]{1,0:T(8,128)(2,1)S(1)}, bf16[128,128]{1,0:T(8,128)(2,1)}, u32[]{:S(2)}) copy-start(bf16[128,128]{1,0:T(8,128)(2,1)} %feat_ref.1) | copy-start | bytes 98308
  5.3 1.2 %copy-start = (bf16[1024,512]{1,0:T(8,128)(2,1)S(1)}, bf16[1024,512]{1,0:T(8,128)(2,1)}, u32[]{:S(2)}) copy-start(bf16[1024,512]{1,0:T(8,128)(2,1)} %place_tiles.1.dense_hbm) | copy-start | bytes 3145732

commit v2 on v1

--- a/solution.py
+++ b/solution.py
@@ -40,26 +40,32 @@
     dense_ref[...] = jnp.zeros_like(dense_ref)
     for index in range(chunks):
         copies[index].wait()
-
-        def place(slot, carry):
-            row = pl.multiple_of(rows_ref[0, slot] * edge, edge)
-            col = pl.multiple_of(cols_ref[0, slot] * edge, edge)
+        for slot in range(index * CHUNK, (index + 1) * CHUNK):
+            live = slot < count
+            row = pl.multiple_of(jnp.where(live, rows_ref[0, slot], 0) * edge, edge)
+            col = pl.multiple_of(jnp.where(live, cols_ref[0, slot], 0) * edge, edge)
             spot = (pl.ds(row, edge), pl.ds(col, edge))
-            dense_ref[spot] = dense_ref[spot] + tiles[slot].astype(F32).astype(BF16)
-            return carry
-
-        first = index * CHUNK
-        last = jnp.clip(count, first, first + CHUNK)
-        lax.fori_loop(first, last, place, 0)
+            tile = tiles[slot] * live.astype(jnp.int32)
+            dense_ref[spot] = dense_ref[spot] + tile.astype(F32).astype(BF16)
+
+
+def finish_kernel(*refs):
+    count = len(refs) // 2
+    sems = refs[-1]
+    copies = [pltpu.make_async_copy(refs[i], refs[count + i], sems.at[i]) for i in range(count)]
+    for copy in copies:
+        copy.start()
+    for copy in copies:
+        copy.wait()
 
 
 def layer_kernel(
     n_row, n_col,
-    feat_ref, cot_ref, self_ref, neigh_ref, deg_ref, dense_hbm,
+    feat_ref, cot_ref, self_ref, neigh_ref, deg_ref, dense,
     hidden_ref, gfeat_ref, gself_ref, gneigh_ref,
-    dense, src, part_out, part_in, gm, back_out, back_in, w_out, w_in, q_out, q_in, fin, back_acc,
-    dense_sem, src_s, src_r, part_s, part_r, gm_s, gm_r, back_s, back_r,
-    w_s, w_r, q_s, q_r, fin_s, fin_r,
+    src, part_out, part_in, gm, back_out, back_in, w_out, w_in, q_out, q_in, p_all, fin, back_acc,
+    src_s, src_r, part_s, part_r, gm_s, gm_r, back_s, back_r,
+    w_s, w_r, q_s, q_r, p_s, p_r, fin_s, fin_r,
 ):
     r = lax.axis_index("row")
     c = lax.axis_index("col")
@@ -81,8 +87,6 @@
             src_ref=source, dst_ref=target, send_sem=send.at[d], recv_sem=recv.at[d],
             device_id=(r, col_at(d)), device_id_type=MESH)
 
-    fetch = pltpu.make_async_copy(dense_hbm, dense, dense_sem)
-    fetch.start()
     barrier = pltpu.get_barrier_semaphore()
     each(1, n_col, lambda d: pl.semaphore_signal(
         barrier, inc=1, device_id=(r, col_at(d)), device_id_type=MESH))
@@ -101,7 +105,6 @@
     across = lax.broadcasted_iota(jnp.int32, (edge, edge), 1)
     inv_col = jnp.sum(jnp.where(down == across, inv_row, 0.0), axis=1, keepdims=True)
     own_linear = dot(feat_ref[...], self_ref[...])
-    fetch.wait()
     keep.wait()
     each(1, n_col, lambda d: src_copy(d).wait_recv())
     source = src[...].reshape(n_col * edge, src.shape[-1])
@@ -136,6 +139,7 @@
     each(1, n_row, lambda d: gm_copy(d).start())
 
     share = w_out.shape[1]
+    used = share // q_out.shape[1]
     both = jnp.concatenate([feat_ref[...], mixed], axis=1)
     w_out[...] = dot(both, grad_linear, ((0,), (0,))).reshape(w_out.shape)
 
@@ -147,16 +151,20 @@
     own_grad = dot(grad_linear, self_ref[...], ((1,), (1,)))
 
     def q_copy(d):
-        return over_row(q_out, q_in.at[d], q_s, q_r, d)
+        return over_row(q_out.at[row_at(d)], q_in.at[d], q_s, q_r, d)
+
+    def p_copy(d):
+        return over_row(p_all.at[r], p_all.at[r], p_s, p_r, d)
 
     def sum_over_col():
         total = w_out[c]
         for d in range(1, n_col):
             w_copy(d).wait_recv()
             total = total + w_in[d]
-        q_out[...] = total.astype(BF16)
+        q_out[:used] = total.reshape((used,) + q_out.shape[1:])
+        if used < n_row:
+            q_out[used:] = jnp.zeros_like(q_out[used:])
         each(1, n_row, lambda d: q_copy(d).start())
-        return total
 
     def back_term(d):
         owner = lax.rem(r - d + n_row, n_row)
@@ -170,7 +178,7 @@
     middle = (n_row + 1) // 2
     back_acc[...] = back_term(0)
     each(1, middle, add_back)
-    total = sum_over_col()
+    sum_over_col()
     each(middle, n_row, add_back)
 
     for b in range(n_col):
@@ -181,15 +189,12 @@
 
     each(1, n_col, lambda d: back_copy(d).start())
 
+    piece = q_out[r]
     for d in range(1, n_row):
         q_copy(d).wait_recv()
-        total = total + q_in[d].astype(F32)
-    fin[c] = total.astype(BF16)
-
-    def fin_copy(d):
-        return over_col(fin.at[c], fin.at[c], fin_s, fin_r, d)
-
-    each(1, n_col, lambda d: fin_copy(d).start())
+        piece = piece + q_in[d]
+    p_all[r] = piece
+    each(1, n_row, lambda d: p_copy(d).start())
 
     returned = back_out[c].astype(F32)
     for d in range(1, n_col):
@@ -197,6 +202,13 @@
         returned = returned + back_in[d].astype(F32)
     gfeat_ref[...] = (own_grad + returned.T).astype(BF16)
 
+    each(1, n_row, lambda d: p_copy(d).wait_recv())
+    fin[c] = p_all[:used].reshape(share, fin.shape[-1]).astype(BF16)
+
+    def fin_copy(d):
+        return over_col(fin.at[c], fin.at[c], fin_s, fin_r, d)
+
+    each(1, n_col, lambda d: fin_copy(d).start())
     each(1, n_col, lambda d: fin_copy(d).wait_recv())
     grads = fin[...].reshape(n_col * share, fin.shape[-1]).astype(F32)
     half = gself_ref.shape[0]
@@ -208,7 +220,7 @@
             copy(d).wait_send()
 
     def drain_row(d):
-        for copy in (part_copy, gm_copy, q_copy):
+        for copy in (part_copy, gm_copy, q_copy, p_copy):
             copy(d).wait_send()
 
     each(1, n_col, drain_col)
@@ -224,17 +236,17 @@
     rows, cols = n_row * edge, n_col * edge
     smem = pl.BlockSpec(memory_space=pltpu.SMEM)
     vmem = pl.BlockSpec(memory_space=pltpu.VMEM)
-    anywhere = pl.BlockSpec(memory_space=pl.ANY)
+    hbm = pl.BlockSpec(memory_space=pltpu.HBM)
     dense = pl.pallas_call(
         functools.partial(place_kernel, chunks),
         out_shape=jax.ShapeDtypeStruct((rows, cols), BF16),
-        in_specs=[smem, smem, smem, anywhere],
+        in_specs=[smem, smem, smem, hbm],
         out_specs=vmem,
         scratch_shapes=[
             pltpu.VMEM((capacity, edge, edge), jnp.int32),
             pltpu.SemaphoreType.DMA((chunks,)),
         ],
-        compiler_params=pltpu.CompilerParams(vmem_limit_bytes=60 * 2**20),
+        compiler_params=pltpu.CompilerParams(vmem_limit_bytes=51 * 2**20),
         name="place_tiles",
     )(
         tile_count.reshape(1, 1),
@@ -243,9 +255,10 @@
         adjacency.reshape(capacity, edge, edge),
     )
     share = 2 * hidden_units // n_col
+    piece = max(share // n_row, 8)
     block = (edge, hidden_units)
     dma = pltpu.SemaphoreType.DMA
-    return pl.pallas_call(
+    results = pl.pallas_call(
         functools.partial(layer_kernel, n_row, n_col),
         out_shape=(
             jax.ShapeDtypeStruct(block, BF16),
@@ -253,10 +266,9 @@
             jax.ShapeDtypeStruct(self_weight.shape, F32),
             jax.ShapeDtypeStruct(neigh_weight.shape, F32),
         ),
-        in_specs=[vmem] * 5 + [anywhere],
+        in_specs=[vmem] * 6,
         out_specs=(vmem,) * 4,
         scratch_shapes=[
-            pltpu.VMEM((rows, cols), BF16),
             pltpu.VMEM((n_col,) + block, BF16),
             pltpu.VMEM((n_row,) + block, BF16),
             pltpu.VMEM((n_row,) + block, BF16),
@@ -265,23 +277,32 @@
             pltpu.VMEM((n_col,) + block, BF16),
             pltpu.VMEM((n_col, share, hidden_units), F32),
             pltpu.VMEM((n_col, share, hidden_units), F32),
-            pltpu.VMEM((share, hidden_units), BF16),
-            pltpu.VMEM((n_row, share, hidden_units), BF16),
+            pltpu.VMEM((n_row, piece, hidden_units), F32),
+            pltpu.VMEM((n_row, piece, hidden_units), F32),
+            pltpu.VMEM((n_row, piece, hidden_units), F32),
             pltpu.VMEM((n_col, share, hidden_units), BF16),
             pltpu.VMEM((hidden_units, cols), F32),
-            dma,
             dma((n_col,)), dma((n_col,)),
             dma((n_row,)), dma((n_row,)),
             dma((n_row,)), dma((n_row,)),
             dma((n_col,)), dma((n_col,)),
             dma((n_col,)), dma((n_col,)),
             dma((n_row,)), dma((n_row,)),
+            dma((n_row,)), dma((n_row,)),
             dma((n_col,)), dma((n_col,)),
         ],
         compiler_params=pltpu.CompilerParams(
-            collective_id=0, has_side_effects=True, vmem_limit_bytes=48 * 2**20),
+            collective_id=0, has_side_effects=True, vmem_limit_bytes=32 * 2**20),
         name="layer_exchange",
     )(features, cotangent, self_weight, neigh_weight, degrees.reshape(1, edge), dense)
+    return pl.pallas_call(
+        finish_kernel,
+        out_shape=tuple(jax.ShapeDtypeStruct(x.shape, x.dtype) for x in results),
+        in_specs=[vmem] * 4,
+        out_specs=(hbm,) * 4,
+        scratch_shapes=[dma((4,))],
+        name="write_outputs",
+    )(*results)
 
 
 def solution(mesh):

time: 42.4 us -> 45.7 us (1.078)
  Pallas kernels: 37 us -> 40.3 us
    pallas_call x1, Pallas kernels: 33.1 us -> 35.8 us  [body(): pl.pallas_call(functools.partial(layer_kernel, n_row, n_col), out_shape=(...]
    pallas_call x0 -> x1, Pallas kernels: none -> 1.62 us  [body(): pl.pallas_call(finish_kernel, out_shape=tuple((jax.ShapeDtypeStruct(x.sha...]
    pallas_call x1, Pallas kernels: 3.93 us -> 2.84 us  [body(): pl.pallas_call(functools.partial(place_kernel, chunks), out_shape=jax.Sha...]
    unnamed x16 -> x22, local copies, waits for them, and re-layouts: 3.73 us -> 3.76 us
where the time goes in v2:
time: 45.7 us; the launch traced here: 45.4 us
  Pallas kernels  40.3 us (88%)
  local copies, waits for them, and re-layouts  3.76 us (8%)
  between operations  1.41 us (3%)
    pallas_call x1, Pallas kernels, body(): pl.pallas_call(functools.partial(layer_kernel, n_row, n_col), out_shape=(...  35.8 us
    unnamed x22, local copies, waits for them, and re-layouts  3.76 us
    pallas_call x1, Pallas kernels, body(): pl.pallas_call(functools.partial(place_kernel, chunks), out_shape=jax.Sha...  2.84 us
    pallas_call x1, Pallas kernels, body(): pl.pallas_call(finish_kernel, out_shape=tuple((jax.ShapeDtypeStruct(x.sha...  1.62 us

profile of v2, /device:TPU:0, one launch (start us, length us, event | category | flops | bytes accessed | tf_op | source)
XLA Modules:
  0.0 45.4 jit_solution(5322074753351560576)
XLA Ops:
  0.6 0.0 copy-start.5
  0.6 0.0 copy-start.4
  0.7 0.0 copy-start.3
  0.7 0.0 copy-start.2
  1.3 0.0 copy-start.8
  1.3 0.6 %copy-done.8 = s32[1,1,64]{2,1,0:T(1,128)S(1)} copy-done((s32[1,1,64]{2,1,0:T(1,128)S(1)}, s32[1,1,64]{2,1,0:T(1,128)}, u32[]{:S(2)}) %copy-start.8) | copy-done | bytes 280
  2.0 0.0 copy-start.9
  2.0 0.7 %copy-done.9 = s32[1,1,64]{2,1,0:T(1,128)S(1)} copy-done((s32[1,1,64]{2,1,0:T(1,128)S(1)}, s32[1,1,64]{2,1,0:T(1,128)}, u32[]{:S(2)}) %copy-start.9) | copy-done | bytes 280
  2.7 0.0 copy-start.10
  2.7 2.8 %place_tiles.1.dense = bf16[1024,512]{1,0:T(8,128)(2,1)S(1)} custom-call(s32[1,1]{1,0:T(1,128)S(6)} %copy.13.count_ref, s32[1,64]{1,0:T(1,128)S(1)} %bitcast.4, s32[1,64]{1,0:T(1,128)S(1)} %bitcast.5, s32[64,128,128]{2,1,0:T(8,128)} %bitcast.7), custom_call_target="tpu_custom_call" | custom-call | tf_op jit(solution)/shard_map/place_tiles/pallas_call | solution.py:240
  5.5 0.0 copy-done.5
  5.5 0.0 copy-done.4
  5.5 0.0 copy-done.3
  5.5 0.0 copy-done.2
  5.5 0.0 copy-done.10
  5.6 35.8 %layer_exchange.1 = (bf16[128,128]{1,0:T(8,128)(2,1)S(1)}, bf16[128,128]{1,0:T(8,128)(2,1)S(1)}, f32[128,128]{1,0:T(8,128)S(1)}, f32[128,128]{1,0:T(8,128)S(1)}) custom-call(bf16[128,128]{1,0:T(8,128)(2,1)S(1)} %copy-done.2, bf16[128,128]{1,0:T(8,128)(2,1)S(1)} %copy-done.3, bf16[128,128]{1,0:T(8,128)(2,1)S(1)} %copy-done.4, bf16[128,128]{1,0:T(8,128)(2,1)S(1)} %copy-done.5, ...), custom_call_target="tpu_custom_call" | custom-call | tf_op jit(solution)/shard_map/layer_exchange/pallas_call | solution.py:261
  41.4 0.0 copy-start
  41.4 0.6 %copy-done = f32[128,128]{1,0:T(8,128)} copy-done((f32[128,128]{1,0:T(8,128)}, f32[128,128]{1,0:T(8,128)S(1)}, u32[]{:S(2)}) %copy-start) | copy-done | bytes 65560
  42.0 0.0 copy-start.1
  42.0 0.6 %copy-done.1 = f32[128,128]{1,0:T(8,128)} copy-done((f32[128,128]{1,0:T(8,128)}, f32[128,128]{1,0:T(8,128)S(1)}, u32[]{:S(2)}) %copy-start.1) | copy-done | bytes 65560
  42.6 0.0 copy-start.6
  42.6 0.6 %copy-done.6 = bf16[128,128]{1,0:T(8,128)(2,1)} copy-done((bf16[128,128]{1,0:T(8,128)(2,1)}, bf16[128,128]{1,0:T(8,128)(2,1)S(1)}, u32[]{:S(2)}) %copy-start.6) | copy-done | bytes 32792
  43.2 0.0 copy-start.7
  43.2 0.6 %copy-done.7 = bf16[128,128]{1,0:T(8,128)(2,1)} copy-done((bf16[128,128]{1,0:T(8,128)(2,1)}, bf16[128,128]{1,0:T(8,128)(2,1)S(1)}, u32[]{:S(2)}) %copy-start.7) | copy-done | bytes 32792
  43.8 1.6 %write_outputs.1 = (bf16[128,128]{1,0:T(8,128)(2,1)}, bf16[128,128]{1,0:T(8,128)(2,1)}, f32[128,128]{1,0:T(8,128)}, f32[128,128]{1,0:T(8,128)}) custom-call(bf16[128,128]{1,0:T(8,128)(2,1)} %copy-done.6, bf16[128,128]{1,0:T(8,128)(2,1)} %copy-done.7, f32[128,128]{1,0:T(8,128)} %copy-done, f32[128,128]{1,0:T(8,128)} %copy-done.1), custom_call_target="tpu_custom_call" | custom-call | tf_op jit(solution)/shard_map/write_outputs/pallas_call | solution.py:298
Async XLA Ops:
  0.6 4.9 %copy-start.5 = (bf16[128,128]{1,0:T(8,128)(2,1)S(1)}, bf16[128,128]{1,0:T(8,128)(2,1)}, u32[]{:S(2)}) copy-start(bf16[128,128]{1,0:T(8,128)(2,1)} %neigh_ref.1) | copy-start | bytes 98308
  0.6 4.9 %copy-start.4 = (bf16[128,128]{1,0:T(8,128)(2,1)S(1)}, bf16[128,128]{1,0:T(8,128)(2,1)}, u32[]{:S(2)}) copy-start(bf16[128,128]{1,0:T(8,128)(2,1)} %self_ref.1) | copy-start | bytes 98308
  0.7 4.9 %copy-start.3 = (bf16[128,128]{1,0:T(8,128)(2,1)S(1)}, bf16[128,128]{1,0:T(8,128)(2,1)}, u32[]{:S(2)}) copy-start(bf16[128,128]{1,0:T(8,128)(2,1)} %cot_ref.1) | copy-start | bytes 98308
  0.7 4.9 %copy-start.2 = (bf16[128,128]{1,0:T(8,128)(2,1)S(1)}, bf16[128,128]{1,0:T(8,128)(2,1)}, u32[]{:S(2)}) copy-start(bf16[128,128]{1,0:T(8,128)(2,1)} %feat_ref.1) | copy-start | bytes 98308
  1.3 0.7 %copy-start.8 = (s32[1,1,64]{2,1,0:T(1,128)S(1)}, s32[1,1,64]{2,1,0:T(1,128)}, u32[]{:S(2)}) copy-start(s32[1,1,64]{2,1,0:T(1,128)} %param.15) | copy-start | bytes 772
  2.0 0.7 %copy-start.9 = (s32[1,1,64]{2,1,0:T(1,128)S(1)}, s32[1,1,64]{2,1,0:T(1,128)}, u32[]{:S(2)}) copy-start(s32[1,1,64]{2,1,0:T(1,128)} %param.16) | copy-start | bytes 772
  2.7 2.9 %copy-start.10 = (s32[128]{0:T(128)S(1)}, s32[128]{0:T(128)}, u32[]{:S(2)}) copy-start(s32[128]{0:T(128)} %param.13) | copy-start | bytes 1540
  41.4 0.6 %copy-start = (f32[128,128]{1,0:T(8,128)}, f32[128,128]{1,0:T(8,128)S(1)}, u32[]{:S(2)}) copy-start(f32[128,128]{1,0:T(8,128)S(1)} %get-tuple-element.10.refs_2_) | copy-start | bytes 196612
  42.0 0.6 %copy-start.1 = (f32[128,128]{1,0:T(8,128)}, f32[128,128]{1,0:T(8,128)S(1)}, u32[]{:S(2)}) copy-start(f32[128,128]{1,0:T(8,128)S(1)} %get-tuple-element.11.refs_3_) | copy-start | bytes 196612
  42.6 0.6 %copy-start.6 = (bf16[128,128]{1,0:T(8,128)(2,1)}, bf16[128,128]{1,0:T(8,128)(2,1)S(1)}, u32[]{:S(2)}) copy-start(bf16[128,128]{1,0:T(8,128)(2,1)S(1)} %get-tuple-element.8.refs_0_) | copy-start | bytes 98308
  43.2 0.6 %copy-start.7 = (bf16[128,128]{1,0:T(8,128)(2,1)}, bf16[128,128]{1,0:T(8,128)(2,1)S(1)}, u32[]{:S(2)}) copy-start(bf16[128,128]{1,0:T(8,128)(2,1)S(1)} %get-tuple-element.9.refs_1_) | copy-start | bytes 98308

commit v3 on v1

--- a/solution.py
+++ b/solution.py
@@ -10,7 +10,7 @@
 MESH = pl.DeviceIdType.MESH
 BF16 = jnp.bfloat16
 F32 = jnp.float32
-CHUNK = 8
+STEP = 4
 
 
 def dot(a, b, contract=((1,), (0,))):
@@ -28,37 +28,22 @@
         lax.fori_loop(low, high, looped, 0)
 
 
-def place_kernel(chunks, count_ref, rows_ref, cols_ref, tiles_hbm, dense_ref, tiles, sems):
-    edge = tiles.shape[-1]
-    copies = []
-    for index in range(chunks):
-        piece = pl.ds(index * CHUNK, CHUNK)
-        copy = pltpu.make_async_copy(tiles_hbm.at[piece], tiles.at[piece], sems.at[index])
+def finish_kernel(*refs):
+    count = len(refs) // 2
+    sems = refs[-1]
+    copies = [pltpu.make_async_copy(refs[i], refs[count + i], sems.at[i]) for i in range(count)]
+    for copy in copies:
         copy.start()
-        copies.append(copy)
-    count = count_ref[0, 0]
-    dense_ref[...] = jnp.zeros_like(dense_ref)
-    for index in range(chunks):
-        copies[index].wait()
-
-        def place(slot, carry):
-            row = pl.multiple_of(rows_ref[0, slot] * edge, edge)
-            col = pl.multiple_of(cols_ref[0, slot] * edge, edge)
-            spot = (pl.ds(row, edge), pl.ds(col, edge))
-            dense_ref[spot] = dense_ref[spot] + tiles[slot].astype(F32).astype(BF16)
-            return carry
-
-        first = index * CHUNK
-        last = jnp.clip(count, first, first + CHUNK)
-        lax.fori_loop(first, last, place, 0)
+    for copy in copies:
+        copy.wait()
 
 
 def layer_kernel(
     n_row, n_col,
-    feat_ref, cot_ref, self_ref, neigh_ref, deg_ref, dense_hbm,
+    order_ref, bounds_ref, feat_ref, cot_ref, self_ref, neigh_ref, deg_ref, tiles_hbm,
     hidden_ref, gfeat_ref, gself_ref, gneigh_ref,
-    dense, src, part_out, part_in, gm, back_out, back_in, w_out, w_in, q_out, q_in, fin, back_acc,
-    dense_sem, src_s, src_r, part_s, part_r, gm_s, gm_r, back_s, back_r,
+    tiles, sums, dense, src, part_out, part_in, gm, back_out, back_in, w_out, w_in, q_out, q_in, fin, back_acc,
+    tiles_r, src_s, src_r, part_s, part_r, gm_s, gm_r, back_s, back_r,
     w_s, w_r, q_s, q_r, fin_s, fin_r,
 ):
     r = lax.axis_index("row")
@@ -81,7 +66,7 @@
             src_ref=source, dst_ref=target, send_sem=send.at[d], recv_sem=recv.at[d],
             device_id=(r, col_at(d)), device_id_type=MESH)
 
-    fetch = pltpu.make_async_copy(dense_hbm, dense, dense_sem)
+    fetch = pltpu.make_async_copy(tiles_hbm, tiles, tiles_r)
     fetch.start()
     barrier = pltpu.get_barrier_semaphore()
     each(1, n_col, lambda d: pl.semaphore_signal(
@@ -102,6 +87,28 @@
     inv_col = jnp.sum(jnp.where(down == across, inv_row, 0.0), axis=1, keepdims=True)
     own_linear = dot(feat_ref[...], self_ref[...])
     fetch.wait()
+
+    capacity = tiles.shape[0]
+    sums[0] = jnp.zeros(sums.shape[1:], BF16)
+
+    def run(step, total):
+        for k in range(STEP):
+            slot = step * STEP + k
+            total = total + tiles[order_ref[0, slot]].astype(F32).astype(BF16)
+            sums[slot + 1] = total
+        return total
+
+    lax.fori_loop(0, capacity // STEP, run, jnp.zeros(sums.shape[1:], BF16))
+
+    def place(row, carry):
+        for col in range(n_col):
+            spot = row * n_col + col
+            rows = pl.ds(pl.multiple_of(row * edge, edge), edge)
+            dense[rows, col * edge:(col + 1) * edge] = (
+                sums[bounds_ref[0, spot + 1]] - sums[bounds_ref[0, spot]])
+        return carry
+
+    lax.fori_loop(0, n_row, place, 0)
     keep.wait()
     each(1, n_col, lambda d: src_copy(d).wait_recv())
     source = src[...].reshape(n_col * edge, src.shape[-1])
@@ -190,7 +197,6 @@
         return over_col(fin.at[c], fin.at[c], fin_s, fin_r, d)
 
     each(1, n_col, lambda d: fin_copy(d).start())
-
     returned = back_out[c].astype(F32)
     for d in range(1, n_col):
         back_copy(d).wait_recv()
@@ -220,32 +226,24 @@
     edge = adjacency.shape[-1]
     capacity = adjacency.shape[2]
     hidden_units = features.shape[-1]
-    chunks = capacity // CHUNK
     rows, cols = n_row * edge, n_col * edge
     smem = pl.BlockSpec(memory_space=pltpu.SMEM)
     vmem = pl.BlockSpec(memory_space=pltpu.VMEM)
-    anywhere = pl.BlockSpec(memory_space=pl.ANY)
-    dense = pl.pallas_call(
-        functools.partial(place_kernel, chunks),
-        out_shape=jax.ShapeDtypeStruct((rows, cols), BF16),
-        in_specs=[smem, smem, smem, anywhere],
-        out_specs=vmem,
-        scratch_shapes=[
-            pltpu.VMEM((capacity, edge, edge), jnp.int32),
-            pltpu.SemaphoreType.DMA((chunks,)),
-        ],
-        compiler_params=pltpu.CompilerParams(vmem_limit_bytes=60 * 2**20),
-        name="place_tiles",
-    )(
-        tile_count.reshape(1, 1),
-        tile_rows.reshape(1, capacity),
-        tile_cols.reshape(1, capacity),
-        adjacency.reshape(capacity, edge, edge),
-    )
+    hbm = pl.BlockSpec(memory_space=pltpu.HBM)
+    places = n_row * n_col
+    slots = jnp.arange(capacity, dtype=jnp.int32)
+    keys = jnp.where(slots < tile_count.reshape(()),
+                     tile_rows.reshape(capacity) * n_col + tile_cols.reshape(capacity), places)
+    spots = jnp.arange(places + 1, dtype=jnp.int32)
+    bounds = jnp.sum((keys[None, :] < spots[:, None]).astype(jnp.int32), axis=1)
+    ahead = (keys[None, :] < keys[:, None]) | (
+        (keys[None, :] == keys[:, None]) & (slots[None, :] < slots[:, None]))
+    rank = jnp.sum(ahead.astype(jnp.int32), axis=1)
+    order = jnp.sum(jnp.where(rank[None, :] == slots[:, None], slots[None, :], 0), axis=1)
     share = 2 * hidden_units // n_col
     block = (edge, hidden_units)
     dma = pltpu.SemaphoreType.DMA
-    return pl.pallas_call(
+    results = pl.pallas_call(
         functools.partial(layer_kernel, n_row, n_col),
         out_shape=(
             jax.ShapeDtypeStruct(block, BF16),
@@ -253,9 +251,11 @@
             jax.ShapeDtypeStruct(self_weight.shape, F32),
             jax.ShapeDtypeStruct(neigh_weight.shape, F32),
         ),
-        in_specs=[vmem] * 5 + [anywhere],
+        in_specs=[smem] * 2 + [vmem] * 5 + [hbm],
         out_specs=(vmem,) * 4,
         scratch_shapes=[
+            pltpu.VMEM((capacity, edge, edge), jnp.int32),
+            pltpu.VMEM((capacity + 1, edge, edge), BF16),
             pltpu.VMEM((rows, cols), BF16),
             pltpu.VMEM((n_col,) + block, BF16),
             pltpu.VMEM((n_row,) + block, BF16),
@@ -279,9 +279,20 @@
             dma((n_col,)), dma((n_col,)),
         ],
         compiler_params=pltpu.CompilerParams(
-            collective_id=0, has_side_effects=True, vmem_limit_bytes=48 * 2**20),
+            collective_id=0, has_side_effects=True, vmem_limit_bytes=58 * 2**20),
         name="layer_exchange",
-    )(features, cotangent, self_weight, neigh_weight, degrees.reshape(1, edge), dense)
+    )(order.reshape(1, capacity), bounds.reshape(1, places + 1), features, cotangent,
+      self_weight, neigh_weight, degrees.reshape(1, edge),
+      adjacency.reshape(capacity, edge, edge))
+    return pl.pallas_call(
+        finish_kernel,
+        out_shape=tuple(jax.ShapeDtypeStruct(x.shape, x.dtype) for x in results),
+        in_specs=[hbm] * 4,
+        out_specs=(hbm,) * 4,
+        scratch_shapes=[dma((4,))],
+        compiler_params=pltpu.CompilerParams(vmem_limit_bytes=60 * 2**20),
+        name="write_outputs",
+    )(*results)
 
 
 def solution(mesh):

time: 42.4 us -> 45.3 us (1.068)
  Pallas kernels: 37 us -> 41.6 us
  local copies, waits for them, and re-layouts: 3.73 us -> 0 us
  other arithmetic: 0 us -> 2.12 us
    unnamed x16 -> x0, local copies, waits for them, and re-layouts: 3.73 us -> none
    pallas_call x1, Pallas kernels: 3.93 us -> 7.1 us  [body(): pl.pallas_call(finish_kernel, out_shape=tuple((jax.ShapeDtypeStruct(x.sha...]
    pallas_call x1, Pallas kernels: 33.1 us -> 34.5 us  [body(): pl.pallas_call(functools.partial(layer_kernel, n_row, n_col), out_shape=(...]
    reduce_sum x0 -> x3, other arithmetic: none -> 1.44 us  [the longest x1 0.64 us: body(): jnp.sum(jnp.where(rank[None, :] == slots[:, None], slots[None, :], 0), ax...]
    select_n x0 -> x1, other arithmetic: none -> 0.68 us  [body(): jnp.where(slots < tile_count.reshape(()), tile_rows.reshape(capacity) * n...]
where the time goes in v3:
time: 45.3 us; the launch traced here: 45 us
  Pallas kernels  41.6 us (92%)
  other arithmetic  2.12 us (5%)
  between operations  1.29 us (3%)
    pallas_call x1, Pallas kernels, body(): pl.pallas_call(functools.partial(layer_kernel, n_row, n_col), out_shape=(...  34.5 us
    pallas_call x1, Pallas kernels, body(): pl.pallas_call(finish_kernel, out_shape=tuple((jax.ShapeDtypeStruct(x.sha...  7.1 us

profile of v3, /device:TPU:0, one launch (start us, length us, event | category | flops | bytes accessed | tf_op | source)
XLA Modules:
  0.0 45.0 jit_solution(2485737481973133460)
XLA Ops:
  1.3 0.7 %compare_select_fusion = s32[64]{0:T(128)S(1)} fusion(s32[1,1,64]{2,1,0:T(1,128)} %param.16, s32[1,1,64]{2,1,0:T(1,128)} %param.15, s32[]{:T(128)} %bitcast.7), kind=kLoop, calls=%fused_computation.8 | loop fusion | flops 256 | bytes 772 | tf_op jit(solution)/shard_map/jit(_where)/select_n | solution.py:235
  2.0 0.6 %convert_reduce_fusion.1 = s32[33]{0:T(128)} fusion(s32[64]{0:T(128)S(1)} %compare_select_fusion), kind=kLoop, calls=%fused_computation.6 | loop fusion | flops 6303 | bytes 388 | tf_op jit(solution)/shard_map/reduce_sum | solution.py:238
  2.6 0.2 convert_reduce_fusion
  2.8 0.6 %select_reduce_fusion = s32[64]{0:T(128)} fusion(s32[64]{0:T(128)S(1)} %convert_reduce_fusion), kind=kLoop, calls=%fused_computation | loop fusion | flops 12224 | bytes 512 | tf_op jit(solution)/shard_map/reduce_sum | solution.py:242
  3.4 34.5 %layer_exchange.1 = (bf16[128,128]{1,0:T(8,128)(2,1)}, bf16[128,128]{1,0:T(8,128)(2,1)}, f32[128,128]{1,0:T(8,128)}, f32[128,128]{1,0:T(8,128)}) custom-call(s32[1,64]{1,0:T(1,128)} %bitcast.11, s32[1,33]{1,0:T(1,128)} %bitcast.10, bf16[128,128]{1,0:T(8,128)(2,1)} %feat_ref.1, bf16[128,128]{1,0:T(8,128)(2,1)} %cot_ref.1, bf16[128,128]{1,0:T(8,128)(2,1)} %self_ref.1, ...), custom_call_target="tpu_custom_call" | custom-call | tf_op jit(solution)/shard_map/layer_exchange/pallas_call | solution.py:246
  38.0 7.1 %write_outputs.1 = (bf16[128,128]{1,0:T(8,128)(2,1)}, bf16[128,128]{1,0:T(8,128)(2,1)}, f32[128,128]{1,0:T(8,128)}, f32[128,128]{1,0:T(8,128)}) custom-call(bf16[128,128]{1,0:T(8,128)(2,1)} %get-tuple-element.8.refs_0_, bf16[128,128]{1,0:T(8,128)(2,1)} %get-tuple-element.9.refs_1_, f32[128,128]{1,0:T(8,128)} %get-tuple-element.10.refs_2_, ...), custom_call_target="tpu_custom_call" | custom-call | tf_op jit(solution)/shard_map/write_outputs/pallas_call | solution.py:287

commit v4 on v3

--- a/solution.py
+++ b/solution.py
@@ -30,20 +30,16 @@
 
 def finish_kernel(*refs):
     count = len(refs) // 2
-    sems = refs[-1]
-    copies = [pltpu.make_async_copy(refs[i], refs[count + i], sems.at[i]) for i in range(count)]
-    for copy in copies:
-        copy.start()
-    for copy in copies:
-        copy.wait()
+    for i in range(count):
+        refs[count + i][...] = refs[i][...]
 
 
 def layer_kernel(
     n_row, n_col,
-    order_ref, bounds_ref, feat_ref, cot_ref, self_ref, neigh_ref, deg_ref, tiles_hbm,
+    count_ref, rows_ref, cols_ref, feat_ref, cot_ref, self_ref, neigh_ref, deg_ref, tiles_hbm,
     hidden_ref, gfeat_ref, gself_ref, gneigh_ref,
-    tiles, sums, dense, src, part_out, part_in, gm, back_out, back_in, w_out, w_in, q_out, q_in, fin, back_acc,
-    tiles_r, src_s, src_r, part_s, part_r, gm_s, gm_r, back_s, back_r,
+    slot_lists, order_ref, bounds_ref, tiles, sums, dense, src, part_out, part_in, gm, back_out, back_in, w_out, w_in, q_out, q_in, fin, back_acc,
+    lists_r, tiles_r, src_s, src_r, part_s, part_r, gm_s, gm_r, back_s, back_r,
     w_s, w_r, q_s, q_r, fin_s, fin_r,
 ):
     r = lax.axis_index("row")
@@ -73,6 +69,24 @@
         barrier, inc=1, device_id=(r, col_at(d)), device_id_type=MESH))
     each(1, n_row, lambda d: pl.semaphore_signal(
         barrier, inc=1, device_id=(row_at(d), c), device_id_type=MESH))
+
+    capacity = tiles.shape[0]
+    places = n_row * n_col
+    slot_down = lax.broadcasted_iota(jnp.int32, (capacity, capacity), 0)
+    slot_across = lax.broadcasted_iota(jnp.int32, (capacity, capacity), 1)
+    key_row = jnp.where(slot_across[:1] < count_ref[...],
+                        rows_ref[...] * n_col + cols_ref[...], places)
+    key_col = jnp.sum(jnp.where(slot_down == slot_across, key_row, 0), axis=1, keepdims=True)
+    ahead = (key_row < key_col) | ((key_row == key_col) & (slot_across < slot_down))
+    rank = jnp.sum(jnp.where(ahead, 1, 0), axis=1, keepdims=True)
+    slot_lists[0:1, :capacity] = jnp.sum(
+        jnp.where(rank == slot_across, slot_down, 0), axis=0, keepdims=True)
+    spots = lax.broadcasted_iota(jnp.int32, (capacity, slot_lists.shape[1]), 1)
+    slot_lists[1:2, :] = jnp.sum(jnp.where(key_col < spots, 1, 0), axis=0, keepdims=True)
+    lists = [pltpu.make_async_copy(slot_lists.at[pl.ds(i, 1)], ref, lists_r.at[i])
+             for i, ref in enumerate((order_ref, bounds_ref))]
+    for copy in lists:
+        copy.start()
     pl.semaphore_wait(barrier, n_row + n_col - 2)
 
     def src_copy(d):
@@ -86,9 +100,10 @@
     across = lax.broadcasted_iota(jnp.int32, (edge, edge), 1)
     inv_col = jnp.sum(jnp.where(down == across, inv_row, 0.0), axis=1, keepdims=True)
     own_linear = dot(feat_ref[...], self_ref[...])
+    for copy in lists:
+        copy.wait()
     fetch.wait()
 
-    capacity = tiles.shape[0]
     sums[0] = jnp.zeros(sums.shape[1:], BF16)
 
     def run(step, total):
@@ -174,11 +189,9 @@
         gm_copy(d).wait_recv()
         back_acc[...] += back_term(d)
 
-    middle = (n_row + 1) // 2
     back_acc[...] = back_term(0)
-    each(1, middle, add_back)
     total = sum_over_col()
-    each(middle, n_row, add_back)
+    each(1, n_row, add_back)
 
     for b in range(n_col):
         back_out[b] = back_acc[:, b * edge:(b + 1) * edge].astype(BF16)
@@ -227,19 +240,9 @@
     capacity = adjacency.shape[2]
     hidden_units = features.shape[-1]
     rows, cols = n_row * edge, n_col * edge
-    smem = pl.BlockSpec(memory_space=pltpu.SMEM)
     vmem = pl.BlockSpec(memory_space=pltpu.VMEM)
     hbm = pl.BlockSpec(memory_space=pltpu.HBM)
-    places = n_row * n_col
-    slots = jnp.arange(capacity, dtype=jnp.int32)
-    keys = jnp.where(slots < tile_count.reshape(()),
-                     tile_rows.reshape(capacity) * n_col + tile_cols.reshape(capacity), places)
-    spots = jnp.arange(places + 1, dtype=jnp.int32)
-    bounds = jnp.sum((keys[None, :] < spots[:, None]).astype(jnp.int32), axis=1)
-    ahead = (keys[None, :] < keys[:, None]) | (
-        (keys[None, :] == keys[:, None]) & (slots[None, :] < slots[:, None]))
-    rank = jnp.sum(ahead.astype(jnp.int32), axis=1)
-    order = jnp.sum(jnp.where(rank[None, :] == slots[:, None], slots[None, :], 0), axis=1)
+    list_width = -(-(n_row * n_col + 1) // 128) * 128
     share = 2 * hidden_units // n_col
     block = (edge, hidden_units)
     dma = pltpu.SemaphoreType.DMA
@@ -251,9 +254,12 @@
             jax.ShapeDtypeStruct(self_weight.shape, F32),
             jax.ShapeDtypeStruct(neigh_weight.shape, F32),
         ),
-        in_specs=[smem] * 2 + [vmem] * 5 + [hbm],
+        in_specs=[vmem] * 8 + [hbm],
         out_specs=(vmem,) * 4,
         scratch_shapes=[
+            pltpu.VMEM((8, list_width), jnp.int32),
+            pltpu.SMEM((1, list_width), jnp.int32),
+            pltpu.SMEM((1, list_width), jnp.int32),
             pltpu.VMEM((capacity, edge, edge), jnp.int32),
             pltpu.VMEM((capacity + 1, edge, edge), BF16),
             pltpu.VMEM((rows, cols), BF16),
@@ -269,6 +275,7 @@
             pltpu.VMEM((n_row, share, hidden_units), BF16),
             pltpu.VMEM((n_col, share, hidden_units), BF16),
             pltpu.VMEM((hidden_units, cols), F32),
+            dma((2,)),
             dma,
             dma((n_col,)), dma((n_col,)),
             dma((n_row,)), dma((n_row,)),
@@ -281,15 +288,14 @@
         compiler_params=pltpu.CompilerParams(
             collective_id=0, has_side_effects=True, vmem_limit_bytes=58 * 2**20),
         name="layer_exchange",
-    )(order.reshape(1, capacity), bounds.reshape(1, places + 1), features, cotangent,
-      self_weight, neigh_weight, degrees.reshape(1, edge),
+    )(tile_count.reshape(1, 1), tile_rows.reshape(1, capacity), tile_cols.reshape(1, capacity),
+      features, cotangent, self_weight, neigh_weight, degrees.reshape(1, edge),
       adjacency.reshape(capacity, edge, edge))
     return pl.pallas_call(
         finish_kernel,
         out_shape=tuple(jax.ShapeDtypeStruct(x.shape, x.dtype) for x in results),
-        in_specs=[hbm] * 4,
-        out_specs=(hbm,) * 4,
-        scratch_shapes=[dma((4,))],
+        in_specs=[vmem] * 4,
+        out_specs=(vmem,) * 4,
         compiler_params=pltpu.CompilerParams(vmem_limit_bytes=60 * 2**20),
         name="write_outputs",
     )(*results)

time: 45.3 us -> 33.9 us (0.75)
  Pallas kernels: 41.6 us -> 32.4 us
  other arithmetic: 2.12 us -> 0 us
    pallas_call x1, Pallas kernels: 7.1 us -> 1.59 us  [body(): pl.pallas_call(finish_kernel, out_shape=tuple((jax.ShapeDtypeStruct(x.sha...]
    pallas_call x1, Pallas kernels: 34.5 us -> 30.8 us  [body(): pl.pallas_call(functools.partial(layer_kernel, n_row, n_col), out_shape=(...]
    reduce_sum x3 -> x0, other arithmetic: 1.44 us -> none  [the longest x1 0.64 us: body(): jnp.sum(jnp.where(rank[None, :] == slots[:, None], slots[None, :], 0), ax...]
    select_n x1 -> x0, other arithmetic: 0.68 us -> none  [body(): jnp.where(slots < tile_count.reshape(()), tile_rows.reshape(capacity) * n...]
where the time goes in v4:
time: 33.9 us; the launch traced here: 33.6 us
  Pallas kernels  32.4 us (96%)
  between operations  1.29 us (4%)
    pallas_call x1, Pallas kernels, body(): pl.pallas_call(functools.partial(layer_kernel, n_row, n_col), out_shape=(...  30.8 us
    pallas_call x1, Pallas kernels, body(): pl.pallas_call(finish_kernel, out_shape=tuple((jax.ShapeDtypeStruct(x.sha...  1.59 us

profile of v4, /device:TPU:0, one launch (start us, length us, event | category | flops | bytes accessed | tf_op | source)
XLA Modules:
  0.0 33.6 jit_solution(14101525913587122433)
XLA Ops:
  1.3 30.8 %layer_exchange.1 = (bf16[128,128]{1,0:T(8,128)(2,1)}, bf16[128,128]{1,0:T(8,128)(2,1)}, f32[128,128]{1,0:T(8,128)}, f32[128,128]{1,0:T(8,128)}) custom-call(s32[1,1]{1,0:T(1,128)S(6)} %copy.13.count_ref, s32[1,64]{1,0:T(1,128)} %bitcast.5, s32[1,64]{1,0:T(1,128)} %bitcast.6, bf16[128,128]{1,0:T(8,128)(2,1)} %feat_ref.1, bf16[128,128]{1,0:T(8,128)(2,1)} %cot_ref.1, ...), custom_call_target="tpu_custom_call" | custom-call | tf_op jit(solution)/shard_map/layer_exchange/pallas_call | solution.py:249
  32.0 1.6 %write_outputs.1 = (bf16[128,128]{1,0:T(8,128)(2,1)}, bf16[128,128]{1,0:T(8,128)(2,1)}, f32[128,128]{1,0:T(8,128)}, f32[128,128]{1,0:T(8,128)}) custom-call(bf16[128,128]{1,0:T(8,128)(2,1)} %get-tuple-element.8.refs_0_, bf16[128,128]{1,0:T(8,128)(2,1)} %get-tuple-element.9.refs_1_, f32[128,128]{1,0:T(8,128)} %get-tuple-element.10.refs_2_, ...), custom_call_target="tpu_custom_call" | custom-call | tf_op jit(solution)/shard_map/write_outputs/pallas_call | solution.py:294

commit v5 on v4

--- a/solution.py
+++ b/solution.py
@@ -38,24 +38,35 @@
     n_row, n_col,
     count_ref, rows_ref, cols_ref, feat_ref, cot_ref, self_ref, neigh_ref, deg_ref, tiles_hbm,
     hidden_ref, gfeat_ref, gself_ref, gneigh_ref,
-    slot_lists, order_ref, bounds_ref, tiles, sums, dense, src, part_out, part_in, gm, back_out, back_in, w_out, w_in, q_out, q_in, fin, back_acc,
-    lists_r, tiles_r, src_s, src_r, part_s, part_r, gm_s, gm_r, back_s, back_r,
-    w_s, w_r, q_s, q_r, fin_s, fin_r,
+    slot_lists, order_ref, bounds_ref, tiles, sums, dense, src, px_out, px_in, pz_out, pz_in, gm, back_out, back_in, w_out, w_in, qx_out, qx_in, qz_out, qz_in, fin, back_acc,
+    lists_r, tiles_r, src_s, src_r, px_s, px_r, pz_s, pz_r, gm_s, gm_r, fw_s, fw_r, back_s, back_r,
+    w_s, w_r, qx_s, qx_r, qz_s, qz_r, fin_s, fin_r,
 ):
     r = lax.axis_index("row")
     c = lax.axis_index("col")
     edge = feat_ref.shape[0]
 
-    def row_at(d):
-        return lax.rem(r + d, n_row)
+    n_line = n_row // 2
+    line, side = r // 2, lax.rem(r, 2)
+
+    def ahead_of(e):
+        return lax.rem(line + e, n_line)
+
+    def behind(e):
+        return lax.rem(line - e + n_line, n_line)
 
     def col_at(d):
         return lax.rem(c + d, n_col)
 
-    def over_row(source, target, send, recv, d):
+    def over_pair(source, target, send, recv):
         return pltpu.make_async_remote_copy(
-            src_ref=source, dst_ref=target, send_sem=send.at[d], recv_sem=recv.at[d],
-            device_id=(row_at(d), c), device_id_type=MESH)
+            src_ref=source, dst_ref=target, send_sem=send, recv_sem=recv,
+            device_id=(line * 2 + 1 - side, c), device_id_type=MESH)
+
+    def over_line(source, target, send, recv, e):
+        return pltpu.make_async_remote_copy(
+            src_ref=source, dst_ref=target, send_sem=send.at[e], recv_sem=recv.at[e],
+            device_id=(ahead_of(e) * 2 + side, c), device_id_type=MESH)
 
     def over_col(source, target, send, recv, d):
         return pltpu.make_async_remote_copy(
@@ -67,8 +78,10 @@
     barrier = pltpu.get_barrier_semaphore()
     each(1, n_col, lambda d: pl.semaphore_signal(
         barrier, inc=1, device_id=(r, col_at(d)), device_id_type=MESH))
-    each(1, n_row, lambda d: pl.semaphore_signal(
-        barrier, inc=1, device_id=(row_at(d), c), device_id_type=MESH))
+    pl.semaphore_signal(
+        barrier, inc=1, device_id=(line * 2 + 1 - side, c), device_id_type=MESH)
+    each(1, n_line, lambda e: pl.semaphore_signal(
+        barrier, inc=1, device_id=(ahead_of(e) * 2 + side, c), device_id_type=MESH))
 
     capacity = tiles.shape[0]
     places = n_row * n_col
@@ -87,7 +100,7 @@
              for i, ref in enumerate((order_ref, bounds_ref))]
     for copy in lists:
         copy.start()
-    pl.semaphore_wait(barrier, n_row + n_col - 2)
+    pl.semaphore_wait(barrier, n_line + n_col - 1)
 
     def src_copy(d):
         return over_col(feat_ref, src.at[c], src_s, src_r, d)
@@ -128,22 +141,35 @@
     each(1, n_col, lambda d: src_copy(d).wait_recv())
     source = src[...].reshape(n_col * edge, src.shape[-1])
 
-    def part_copy(d):
-        return over_row(part_out.at[d], part_in.at[d], part_s, part_r, d)
-
-    def partial(d):
-        rows = pl.ds(pl.multiple_of(row_at(d) * edge, edge), edge)
+    def px_copy(e):
+        return over_pair(px_out.at[e], px_in.at[e], px_s.at[e], px_r.at[e])
+
+    def pz_copy(e):
+        return over_line(pz_out.at[e], pz_in.at[e], pz_s, pz_r, e)
+
+    def partial(e, which):
+        rows = pl.ds(pl.multiple_of((ahead_of(e) * 2 + which) * edge, edge), edge)
         return dot(dense[rows, :], source)
 
-    def send_part(d):
-        part_out[d] = partial(d).astype(BF16)
-        part_copy(d).start()
-
-    each(1, n_row, send_part)
-    agg = partial(0).astype(BF16).astype(F32)
-    for d in range(1, n_row):
-        part_copy(d).wait_recv()
-        agg = agg + part_in[d].astype(F32)
+    def send_px(e):
+        px_out[e] = partial(e, 1 - side).astype(BF16)
+        px_copy(e).start()
+
+    def send_pz(e):
+        own = partial(e, side)
+        px_copy(e).wait_recv()
+        pz_out[e] = (own + px_in[e].astype(F32)).astype(BF16)
+        pz_copy(e).start()
+
+    each(1, n_line, send_px)
+    send_px(0)
+    each(1, n_line, send_pz)
+    agg = partial(0, side)
+    px_copy(0).wait_recv()
+    agg = agg + px_in[0].astype(F32)
+    for e in range(1, n_line):
+        pz_copy(e).wait_recv()
+        agg = agg + pz_in[e].astype(F32)
 
     mixed = (agg * inv_col).astype(BF16)
     linear = own_linear + dot(mixed, neigh_ref[...])
@@ -152,10 +178,15 @@
     grad_linear = (cot_ref[...].astype(F32) * slope).astype(BF16)
     gm[r] = (dot(neigh_ref[...], grad_linear, ((1,), (1,))) * inv_row).astype(BF16)
 
-    def gm_copy(d):
-        return over_row(gm.at[r], gm.at[r], gm_s, gm_r, d)
-
-    each(1, n_row, lambda d: gm_copy(d).start())
+    def gm_copy(e):
+        return over_line(gm.at[r], gm.at[r], gm_s, gm_r, e)
+
+    def fw_copy(e):
+        block = gm.at[behind(e) * 2 + side]
+        return over_pair(block, block, fw_s.at[e], fw_r.at[e])
+
+    each(1, n_line, lambda e: gm_copy(e).start())
+    fw_copy(0).start()
 
     share = w_out.shape[1]
     both = jnp.concatenate([feat_ref[...], mixed], axis=1)
@@ -168,30 +199,45 @@
     hidden_ref[...] = (linear * sigma).astype(BF16)
     own_grad = dot(grad_linear, self_ref[...], ((1,), (1,)))
 
-    def q_copy(d):
-        return over_row(q_out, q_in.at[d], q_s, q_r, d)
-
-    def sum_over_col():
-        total = w_out[c]
-        for d in range(1, n_col):
-            w_copy(d).wait_recv()
-            total = total + w_in[d]
-        q_out[...] = total.astype(BF16)
-        each(1, n_row, lambda d: q_copy(d).start())
-        return total
-
-    def back_term(d):
-        owner = lax.rem(r - d + n_row, n_row)
-        rows = pl.ds(pl.multiple_of(owner * edge, edge), edge)
-        return dot(gm[owner], dense[rows, :])
-
-    def add_back(d):
-        gm_copy(d).wait_recv()
-        back_acc[...] += back_term(d)
-
+    qx_copy = over_pair(qx_out, qx_in, qx_s, qx_r)
+
+    def qz_copy(e):
+        return over_line(qz_out, qz_in.at[e], qz_s, qz_r, e)
+
+    def forward(e):
+        gm_copy(e).wait_recv()
+        fw_copy(e).start()
+
+    def back_term(e):
+        fw_copy(e).wait_recv()
+        first = behind(e) * 2
+        rows = pl.ds(pl.multiple_of(first * edge, 2 * edge), 2 * edge)
+        return dot(jnp.concatenate([gm[first], gm[first + 1]], axis=1), dense[rows, :])
+
+    def add_back(e):
+        back_acc[...] += back_term(e)
+
+    forward(1)
+    total = w_out[c]
+    for d in range(1, n_col):
+        w_copy(d).wait_recv()
+        total = total + w_in[d]
+    qx_out[...] = total.astype(BF16)
+    qx_copy.start()
     back_acc[...] = back_term(0)
-    total = sum_over_col()
-    each(1, n_row, add_back)
+    forward(2)
+    add_back(1)
+    qx_copy.wait_recv()
+    total = total + qx_in[...].astype(F32)
+    qz_out[...] = total.astype(BF16)
+    each(1, n_line, lambda e: qz_copy(e).start())
+
+    def forward_and_add(e):
+        forward(e)
+        add_back(e - 1)
+
+    each(3, n_line, forward_and_add)
+    add_back(n_line - 1)
 
     for b in range(n_col):
         back_out[b] = back_acc[:, b * edge:(b + 1) * edge].astype(BF16)
@@ -201,9 +247,9 @@
 
     each(1, n_col, lambda d: back_copy(d).start())
 
-    for d in range(1, n_row):
-        q_copy(d).wait_recv()
-        total = total + q_in[d].astype(F32)
+    for e in range(1, n_line):
+        qz_copy(e).wait_recv()
+        total = total + qz_in[e].astype(F32)
     fin[c] = total.astype(BF16)
 
     def fin_copy(d):
@@ -226,12 +272,14 @@
         for copy in (src_copy, w_copy, back_copy, fin_copy):
             copy(d).wait_send()
 
-    def drain_row(d):
-        for copy in (part_copy, gm_copy, q_copy):
-            copy(d).wait_send()
+    def drain_line(e):
+        for copy in (px_copy, pz_copy, gm_copy, fw_copy, qz_copy):
+            copy(e).wait_send()
 
     each(1, n_col, drain_col)
-    each(1, n_row, drain_row)
+    each(1, n_line, drain_line)
+    for copy in (px_copy(0), fw_copy(0), qx_copy):
+        copy.wait_send()
 
 
 def body(n_row, n_col, features, cotangent, self_weight, neigh_weight, degrees,
@@ -244,6 +292,7 @@
     hbm = pl.BlockSpec(memory_space=pltpu.HBM)
     list_width = -(-(n_row * n_col + 1) // 128) * 128
     share = 2 * hidden_units // n_col
+    n_line = n_row // 2
     block = (edge, hidden_units)
     dma = pltpu.SemaphoreType.DMA
     results = pl.pallas_call(
@@ -264,25 +313,32 @@
             pltpu.VMEM((capacity + 1, edge, edge), BF16),
             pltpu.VMEM((rows, cols), BF16),
             pltpu.VMEM((n_col,) + block, BF16),
-            pltpu.VMEM((n_row,) + block, BF16),
-            pltpu.VMEM((n_row,) + block, BF16),
+            pltpu.VMEM((n_line,) + block, BF16),
+            pltpu.VMEM((n_line,) + block, BF16),
+            pltpu.VMEM((n_line,) + block, BF16),
+            pltpu.VMEM((n_line,) + block, BF16),
             pltpu.VMEM((n_row,) + block, BF16),
             pltpu.VMEM((n_col,) + block, BF16),
             pltpu.VMEM((n_col,) + block, BF16),
             pltpu.VMEM((n_col, share, hidden_units), F32),
             pltpu.VMEM((n_col, share, hidden_units), F32),
             pltpu.VMEM((share, hidden_units), BF16),
-            pltpu.VMEM((n_row, share, hidden_units), BF16),
+            pltpu.VMEM((share, hidden_units), BF16),
+            pltpu.VMEM((share, hidden_units), BF16),
+            pltpu.VMEM((n_line, share, hidden_units), BF16),
             pltpu.VMEM((n_col, share, hidden_units), BF16),
             pltpu.VMEM((hidden_units, cols), F32),
             dma((2,)),
             dma,
             dma((n_col,)), dma((n_col,)),
-            dma((n_row,)), dma((n_row,)),
-            dma((n_row,)), dma((n_row,)),
+            dma((n_line,)), dma((n_line,)),
+            dma((n_line,)), dma((n_line,)),
+            dma((n_line,)), dma((n_line,)),
+            dma((n_line,)), dma((n_line,)),
             dma((n_col,)), dma((n_col,)),
             dma((n_col,)), dma((n_col,)),
-            dma((n_row,)), dma((n_row,)),
+            dma, dma,
+            dma((n_line,)), dma((n_line,)),
             dma((n_col,)), dma((n_col,)),
         ],
         compiler_params=pltpu.CompilerParams(

time: 33.9 us -> 36.2 us (1.068)
  Pallas kernels: 32.4 us -> 34.7 us
    pallas_call x1, Pallas kernels: 30.8 us -> 33.1 us  [body(): pl.pallas_call(functools.partial(layer_kernel, n_row, n_col), out_shape=(...]
where the time goes in v5:
time: 36.2 us; the launch traced here: 36 us
  Pallas kernels  34.7 us (96%)
  between operations  1.29 us (4%)
    pallas_call x1, Pallas kernels, body(): pl.pallas_call(functools.partial(layer_kernel, n_row, n_col), out_shape=(...  33.1 us
    pallas_call x1, Pallas kernels, body(): pl.pallas_call(finish_kernel, out_shape=tuple((jax.ShapeDtypeStruct(x.sha...  1.59 us

profile of v5, /device:TPU:0, one launch (start us, length us, event | category | flops | bytes accessed | tf_op | source)
XLA Modules:
  0.0 36.0 jit_solution(2912200082865685656)
XLA Ops:
  1.3 33.1 %layer_exchange.1 = (bf16[128,128]{1,0:T(8,128)(2,1)}, bf16[128,128]{1,0:T(8,128)(2,1)}, f32[128,128]{1,0:T(8,128)}, f32[128,128]{1,0:T(8,128)}) custom-call(s32[1,1]{1,0:T(1,128)S(6)} %copy.13.count_ref, s32[1,64]{1,0:T(1,128)} %bitcast.5, s32[1,64]{1,0:T(1,128)} %bitcast.6, bf16[128,128]{1,0:T(8,128)(2,1)} %feat_ref.1, bf16[128,128]{1,0:T(8,128)(2,1)} %cot_ref.1, ...), custom_call_target="tpu_custom_call" | custom-call | tf_op jit(solution)/shard_map/layer_exchange/pallas_call | solution.py:298
  34.4 1.6 %write_outputs.1 = (bf16[128,128]{1,0:T(8,128)(2,1)}, bf16[128,128]{1,0:T(8,128)(2,1)}, f32[128,128]{1,0:T(8,128)}, f32[128,128]{1,0:T(8,128)}) custom-call(bf16[128,128]{1,0:T(8,128)(2,1)} %get-tuple-element.8.refs_0_, bf16[128,128]{1,0:T(8,128)(2,1)} %get-tuple-element.9.refs_1_, f32[128,128]{1,0:T(8,128)} %get-tuple-element.10.refs_2_, ...), custom_call_target="tpu_custom_call" | custom-call | tf_op jit(solution)/shard_map/write_outputs/pallas_call | solution.py:350

commit v6 on v4

--- a/solution.py
+++ b/solution.py
@@ -46,8 +46,20 @@
     c = lax.axis_index("col")
     edge = feat_ref.shape[0]
 
-    def row_at(d):
-        return lax.rem(r + d, n_row)
+    def row_at(m):
+        other, bit = 0, 1
+        while bit < n_row:
+            other = other + bit * (((r // bit) + (m // bit)) % 2)
+            bit *= 2
+        return other
+
+    def far_first(step):
+        each(1, n_row, lambda d: step(n_row - d))
+
+    def near_first(step):
+        half = n_row // 2
+        each(1, half, step)
+        each(0, half, lambda d: step(n_row - 1 - d))
 
     def col_at(d):
         return lax.rem(c + d, n_col)
@@ -139,7 +151,7 @@
         part_out[d] = partial(d).astype(BF16)
         part_copy(d).start()
 
-    each(1, n_row, send_part)
+    far_first(send_part)
     agg = partial(0).astype(BF16).astype(F32)
     for d in range(1, n_row):
         part_copy(d).wait_recv()
@@ -155,7 +167,7 @@
     def gm_copy(d):
         return over_row(gm.at[r], gm.at[r], gm_s, gm_r, d)
 
-    each(1, n_row, lambda d: gm_copy(d).start())
+    far_first(lambda d: gm_copy(d).start())
 
     share = w_out.shape[1]
     both = jnp.concatenate([feat_ref[...], mixed], axis=1)
@@ -177,11 +189,11 @@
             w_copy(d).wait_recv()
             total = total + w_in[d]
         q_out[...] = total.astype(BF16)
-        each(1, n_row, lambda d: q_copy(d).start())
+        far_first(lambda d: q_copy(d).start())
         return total
 
     def back_term(d):
-        owner = lax.rem(r - d + n_row, n_row)
+        owner = row_at(d)
         rows = pl.ds(pl.multiple_of(owner * edge, edge), edge)
         return dot(gm[owner], dense[rows, :])
 
@@ -191,7 +203,7 @@
 
     back_acc[...] = back_term(0)
     total = sum_over_col()
-    each(1, n_row, add_back)
+    near_first(add_back)
 
     for b in range(n_col):
         back_out[b] = back_acc[:, b * edge:(b + 1) * edge].astype(BF16)

time: 33.9 us -> 33.9 us (level)
  no operation moved by 1% of the time
where the time goes in v6:
time: 33.9 us; the launch traced here: 33.6 us
  Pallas kernels  32.3 us (95%)
  between operations  1.29 us (4%)
    pallas_call x1, Pallas kernels, body(): pl.pallas_call(functools.partial(layer_kernel, n_row, n_col), out_shape=(...  30.7 us
    pallas_call x1, Pallas kernels, body(): pl.pallas_call(finish_kernel, out_shape=tuple((jax.ShapeDtypeStruct(x.sha...  1.59 us

profile of v6, /device:TPU:0, one launch (start us, length us, event | category | flops | bytes accessed | tf_op | source)
XLA Modules:
  0.0 33.6 jit_solution(14802254987165327487)
XLA Ops:
  1.3 30.7 %layer_exchange.1 = (bf16[128,128]{1,0:T(8,128)(2,1)}, bf16[128,128]{1,0:T(8,128)(2,1)}, f32[128,128]{1,0:T(8,128)}, f32[128,128]{1,0:T(8,128)}) custom-call(s32[1,1]{1,0:T(1,128)S(6)} %copy.13.count_ref, s32[1,64]{1,0:T(1,128)} %bitcast.5, s32[1,64]{1,0:T(1,128)} %bitcast.6, bf16[128,128]{1,0:T(8,128)(2,1)} %feat_ref.1, bf16[128,128]{1,0:T(8,128)(2,1)} %cot_ref.1, ...), custom_call_target="tpu_custom_call" | custom-call | tf_op jit(solution)/shard_map/layer_exchange/pallas_call | solution.py:261
  32.0 1.6 %write_outputs.1 = (bf16[128,128]{1,0:T(8,128)(2,1)}, bf16[128,128]{1,0:T(8,128)(2,1)}, f32[128,128]{1,0:T(8,128)}, f32[128,128]{1,0:T(8,128)}) custom-call(bf16[128,128]{1,0:T(8,128)(2,1)} %get-tuple-element.8.refs_0_, bf16[128,128]{1,0:T(8,128)(2,1)} %get-tuple-element.9.refs_1_, f32[128,128]{1,0:T(8,128)} %get-tuple-element.10.refs_2_, ...), custom_call_target="tpu_custom_call" | custom-call | tf_op jit(solution)/shard_map/write_outputs/pallas_call | solution.py:306

commit v7 on v4

--- a/solution.py
+++ b/solution.py
@@ -46,8 +46,11 @@
     c = lax.axis_index("col")
     edge = feat_ref.shape[0]
 
+    n_line = n_row // 2
+    line, side = r // 2, lax.rem(r, 2)
+
     def row_at(d):
-        return lax.rem(r + d, n_row)
+        return lax.rem(line + d // 2, n_line) * 2 + lax.rem(side + d % 2, 2)
 
     def col_at(d):
         return lax.rem(c + d, n_col)
@@ -129,18 +132,24 @@
     source = src[...].reshape(n_col * edge, src.shape[-1])
 
     def part_copy(d):
-        return over_row(part_out.at[d], part_in.at[d], part_s, part_r, d)
-
-    def partial(d):
-        rows = pl.ds(pl.multiple_of(row_at(d) * edge, edge), edge)
-        return dot(dense[rows, :], source)
-
-    def send_part(d):
-        part_out[d] = partial(d).astype(BF16)
-        part_copy(d).start()
-
-    each(1, n_row, send_part)
-    agg = partial(0).astype(BF16).astype(F32)
+        leaving = part_out.at[d // 2 * 2 + lax.rem(side + d % 2, 2)]
+        return over_row(leaving, part_in.at[d], part_s, part_r, d)
+
+    def partial(e):
+        first = lax.rem(line + e, n_line) * 2
+        rows = pl.ds(pl.multiple_of(first * edge, 2 * edge), 2 * edge)
+        pair = dot(dense[rows, :], source).astype(BF16)
+        part_out[pl.ds(2 * e, 2)] = pair.reshape((2,) + part_out.shape[1:])
+
+    def send_part(e):
+        partial(e)
+        part_copy(2 * e).start()
+        part_copy(2 * e + 1).start()
+
+    each(1, n_line, send_part)
+    partial(0)
+    part_copy(1).start()
+    agg = part_out[side].astype(F32)
     for d in range(1, n_row):
         part_copy(d).wait_recv()
         agg = agg + part_in[d].astype(F32)
@@ -150,13 +159,6 @@
     sigma = jax.nn.sigmoid(linear)
     slope = sigma * (1.0 + linear * (1.0 - sigma))
     grad_linear = (cot_ref[...].astype(F32) * slope).astype(BF16)
-    gm[r] = (dot(neigh_ref[...], grad_linear, ((1,), (1,))) * inv_row).astype(BF16)
-
-    def gm_copy(d):
-        return over_row(gm.at[r], gm.at[r], gm_s, gm_r, d)
-
-    each(1, n_row, lambda d: gm_copy(d).start())
-
     share = w_out.shape[1]
     both = jnp.concatenate([feat_ref[...], mixed], axis=1)
     w_out[...] = dot(both, grad_linear, ((0,), (0,))).reshape(w_out.shape)
@@ -165,6 +167,12 @@
         return over_col(w_out.at[col_at(d)], w_in.at[d], w_s, w_r, d)
 
     each(1, n_col, lambda d: w_copy(d).start())
+    gm[r] = (dot(neigh_ref[...], grad_linear, ((1,), (1,))) * inv_row).astype(BF16)
+
+    def gm_copy(d):
+        return over_row(gm.at[r], gm.at[r], gm_s, gm_r, d)
+
+    each(1, n_row, lambda d: gm_copy(d).start())
     hidden_ref[...] = (linear * sigma).astype(BF16)
     own_grad = dot(grad_linear, self_ref[...], ((1,), (1,)))
 
@@ -180,18 +188,20 @@
         each(1, n_row, lambda d: q_copy(d).start())
         return total
 
-    def back_term(d):
-        owner = lax.rem(r - d + n_row, n_row)
-        rows = pl.ds(pl.multiple_of(owner * edge, edge), edge)
-        return dot(gm[owner], dense[rows, :])
-
-    def add_back(d):
-        gm_copy(d).wait_recv()
-        back_acc[...] += back_term(d)
-
+    def back_term(e):
+        first = lax.rem(line - e + n_line, n_line) * 2
+        rows = pl.ds(pl.multiple_of(first * edge, 2 * edge), 2 * edge)
+        return dot(jnp.concatenate([gm[first], gm[first + 1]], axis=1), dense[rows, :])
+
+    def add_back(e):
+        gm_copy(2 * e).wait_recv()
+        gm_copy(2 * e + 1).wait_recv()
+        back_acc[...] += back_term(e)
+
+    total = sum_over_col()
+    gm_copy(1).wait_recv()
     back_acc[...] = back_term(0)
-    total = sum_over_col()
-    each(1, n_row, add_back)
+    each(1, n_line, add_back)
 
     for b in range(n_col):
         back_out[b] = back_acc[:, b * edge:(b + 1) * edge].astype(BF16)

time: 33.9 us -> 33.8 us (level)
  no operation moved by 1% of the time
where the time goes in v7:
time: 33.8 us; the launch traced here: 33.5 us
  Pallas kernels  32.2 us (95%)
  between operations  1.29 us (4%)
    pallas_call x1, Pallas kernels, body(): pl.pallas_call(functools.partial(layer_kernel, n_row, n_col), out_shape=(...  30.7 us
    pallas_call x1, Pallas kernels, body(): pl.pallas_call(finish_kernel, out_shape=tuple((jax.ShapeDtypeStruct(x.sha...  1.59 us

profile of v7, /device:TPU:0, one launch (start us, length us, event | category | flops | bytes accessed | tf_op | source)
XLA Modules:
  0.0 33.5 jit_solution(915377499383891515)
XLA Ops:
  1.3 30.7 %layer_exchange.1 = (bf16[128,128]{1,0:T(8,128)(2,1)}, bf16[128,128]{1,0:T(8,128)(2,1)}, f32[128,128]{1,0:T(8,128)}, f32[128,128]{1,0:T(8,128)}) custom-call(s32[1,1]{1,0:T(1,128)S(6)} %copy.13.count_ref, s32[1,64]{1,0:T(1,128)} %bitcast.5, s32[1,64]{1,0:T(1,128)} %bitcast.6, bf16[128,128]{1,0:T(8,128)(2,1)} %feat_ref.1, bf16[128,128]{1,0:T(8,128)(2,1)} %cot_ref.1, ...), custom_call_target="tpu_custom_call" | custom-call | tf_op jit(solution)/shard_map/layer_exchange/pallas_call | solution.py:259
  31.9 1.6 %write_outputs.1 = (bf16[128,128]{1,0:T(8,128)(2,1)}, bf16[128,128]{1,0:T(8,128)(2,1)}, f32[128,128]{1,0:T(8,128)}, f32[128,128]{1,0:T(8,128)}) custom-call(bf16[128,128]{1,0:T(8,128)(2,1)} %get-tuple-element.8.refs_0_, bf16[128,128]{1,0:T(8,128)(2,1)} %get-tuple-element.9.refs_1_, f32[128,128]{1,0:T(8,128)} %get-tuple-element.10.refs_2_, ...), custom_call_target="tpu_custom_call" | custom-call | tf_op jit(solution)/shard_map/write_outputs/pallas_call | solution.py:304

commit v8 on v7

--- a/solution.py
+++ b/solution.py
@@ -90,6 +90,20 @@
              for i, ref in enumerate((order_ref, bounds_ref))]
     for copy in lists:
         copy.start()
+    for copy in lists:
+        copy.wait()
+    fetch.wait()
+
+    sums[0] = jnp.zeros(sums.shape[1:], BF16)
+
+    def run(step, total):
+        for k in range(STEP):
+            slot = step * STEP + k
+            total = total + tiles[order_ref[0, slot]].astype(F32).astype(BF16)
+            sums[slot + 1] = total
+        return total
+
+    lax.fori_loop(0, capacity // STEP, run, jnp.zeros(sums.shape[1:], BF16))
     pl.semaphore_wait(barrier, n_row + n_col - 2)
 
     def src_copy(d):
@@ -103,21 +117,6 @@
     across = lax.broadcasted_iota(jnp.int32, (edge, edge), 1)
     inv_col = jnp.sum(jnp.where(down == across, inv_row, 0.0), axis=1, keepdims=True)
     own_linear = dot(feat_ref[...], self_ref[...])
-    for copy in lists:
-        copy.wait()
-    fetch.wait()
-
-    sums[0] = jnp.zeros(sums.shape[1:], BF16)
-
-    def run(step, total):
-        for k in range(STEP):
-            slot = step * STEP + k
-            total = total + tiles[order_ref[0, slot]].astype(F32).astype(BF16)
-            sums[slot + 1] = total
-        return total
-
-    lax.fori_loop(0, capacity // STEP, run, jnp.zeros(sums.shape[1:], BF16))
-
     def place(row, carry):
         for col in range(n_col):
             spot = row * n_col + col

time: 33.8 us -> 35 us (1.036)
  Pallas kernels: 32.2 us -> 33.4 us
    pallas_call x1, Pallas kernels: 30.7 us -> 31.8 us  [body(): pl.pallas_call(functools.partial(layer_kernel, n_row, n_col), out_shape=(...]
where the time goes in v8:
time: 35 us; the launch traced here: 34.7 us
  Pallas kernels  33.4 us (95%)
  between operations  1.29 us (4%)
    pallas_call x1, Pallas kernels, body(): pl.pallas_call(functools.partial(layer_kernel, n_row, n_col), out_shape=(...  31.8 us
    pallas_call x1, Pallas kernels, body(): pl.pallas_call(finish_kernel, out_shape=tuple((jax.ShapeDtypeStruct(x.sha...  1.59 us

profile of v8, /device:TPU:0, one launch (start us, length us, event | category | flops | bytes accessed | tf_op | source)
XLA Modules:
  0.0 34.7 jit_solution(6255272017634492497)
XLA Ops:
  1.3 31.8 %layer_exchange.1 = (bf16[128,128]{1,0:T(8,128)(2,1)}, bf16[128,128]{1,0:T(8,128)(2,1)}, f32[128,128]{1,0:T(8,128)}, f32[128,128]{1,0:T(8,128)}) custom-call(s32[1,1]{1,0:T(1,128)S(6)} %copy.13.count_ref, s32[1,64]{1,0:T(1,128)} %bitcast.5, s32[1,64]{1,0:T(1,128)} %bitcast.6, bf16[128,128]{1,0:T(8,128)(2,1)} %feat_ref.1, bf16[128,128]{1,0:T(8,128)(2,1)} %cot_ref.1, ...), custom_call_target="tpu_custom_call" | custom-call | tf_op jit(solution)/shard_map/layer_exchange/pallas_call | solution.py:258
  33.1 1.6 %write_outputs.1 = (bf16[128,128]{1,0:T(8,128)(2,1)}, bf16[128,128]{1,0:T(8,128)(2,1)}, f32[128,128]{1,0:T(8,128)}, f32[128,128]{1,0:T(8,128)}) custom-call(bf16[128,128]{1,0:T(8,128)(2,1)} %get-tuple-element.8.refs_0_, bf16[128,128]{1,0:T(8,128)(2,1)} %get-tuple-element.9.refs_1_, f32[128,128]{1,0:T(8,128)} %get-tuple-element.10.refs_2_, ...), custom_call_target="tpu_custom_call" | custom-call | tf_op jit(solution)/shard_map/write_outputs/pallas_call | solution.py:303
